TPU v7x, 512 devices: a whole 4x4x16 slice. The times are simulated.
512 devices in a mesh: side: 2 (over x_hi), row: 16 (over z), col: 16 (over x_lo, y, core).
Axes of the slice: x: 4 (x_hi: 2, x_lo: 2; x = x_hi * 2 + x_lo), y: 4, z: 16, core: 2. Of those that a mesh axis runs over, the one named last changes fastest.
Arguments:
- query: bfloat16 [2, 32, 4096], P(None, 'row'), may hold values from -32 to 32
- new_keys: bfloat16 [2, 32, 512], P(None, 'row'), may hold values from -6 to 6
- new_values: bfloat16 [2, 32, 512], P(None, 'row'), may hold values from -12 to 12
- key_cache: bfloat16 [32, 6144, 512], P('row', 'col'), may hold values from -4 to 4
- value_cache: bfloat16 [32, 6144, 512], P('row', 'col'), may hold values from -12 to 12
- lengths: int32 [32], P('row'), may hold values from 1024 to 6144, as said below
- residual: bfloat16 [2, 32, 8192], P(None, None, 'row'), may hold values from -32 to 32
- out_weight: bfloat16 [4096, 8192], P('col', 'row'), may hold values from -0.5 to 0.5
- norm_gain: bfloat16 [8192], P('row'), may hold values from 0.099609375 to 1.8984375
- gate_weight: bfloat16 [8192, 14336], P('row', 'col'), may hold values from -0.0625 to 0.0625
- up_weight: bfloat16 [8192, 14336], P('row', 'col'), may hold values from -0.0625 to 0.0625
- down_weight: bfloat16 [14336, 8192], P('col', 'row'), may hold values from -0.046875 to 0.046875
Outputs:
- hidden_out: bfloat16 [2, 32, 8192], P(None, None, 'row')
Inputs may be any that keep to these rules, and one draw needn't show every extreme that they name: `lengths`: every value from 1024 to 6144 can occur; in every draw some row has exactly 6144 and some row exactly 1024.
All inputs are finite; a program needn't handle non-finite values.
Results may differ from a plain program's by a relative error of at most 0.0059.
Values may be sent and summed in bfloat16 or wider, within the bound.
A program may use at most 64 MiB of HBM per device.

v0:
```python
import math

import jax
import jax.numpy as jnp
from jax import lax
from jax.sharding import PartitionSpec as P

D = 8192
HEADS = 32
KV_HEADS = 4
HD = 128


very_low = -1e30


def partner(value, axis, bit):
    mask = 2**bit
    pairs = [(source, source ^ mask) for source in range(lax.axis_size(axis))]
    return lax.ppermute(value, axis, pairs)


def joined(part, axis, combine):
    gathered = jax.tree.map(lambda a: lax.all_gather(a, axis), part)

    def take(source):
        return jax.tree.map(lambda a: lax.dynamic_index_in_dim(a, source, 0, False), gathered)

    return lax.fori_loop(
        1, lax.axis_size(axis), lambda source, state: combine(state, take(source)), take(0)
    )


def combine(first, second):
    peak_a, total_a, summed_a = first
    peak_b, total_b, summed_b = second
    peak = jnp.maximum(peak_a, peak_b)
    scale_a = jnp.exp(peak_a - peak)
    scale_b = jnp.exp(peak_b - peak)
    return (
        peak,
        total_a * scale_a + total_b * scale_b,
        summed_a * scale_a[..., None] + summed_b * scale_b[..., None],
    )


def cross(value):
    return partner(value, "side", 0)


def tile_sum(value):
    return lax.psum(value, "col")


def partial_softmax(queries, keys_part, values_part, live_part):
    scores = jnp.einsum(
        "bkgd,bpkd->bkgp", queries, keys_part, preferred_element_type=jnp.float32
    ) * (1.0 / math.sqrt(queries.shape[-1]))
    scores = jnp.where(live_part[:, None, None, :], scores, very_low)
    peak = jnp.max(scores, axis=-1)
    weights = jnp.where(live_part[:, None, None, :], jnp.exp(scores - peak[..., None]), 0.0)
    summed = jnp.einsum(
        "bkgp,bpkd->bkgd", weights, values_part.astype(jnp.float32), precision=lax.Precision.HIGHEST
    )
    return (peak, jnp.sum(weights, axis=-1), summed)


def shards(
    query,
    new_keys,
    new_values,
    key_cache,
    value_cache,
    lengths,
    residual,
    out_weight,
    norm_gain,
    gate_weight,
    up_weight,
    down_weight,
):
    side_index = lax.axis_index("side")
    serving = side_index == 0
    ffn_side = jnp.logical_not(serving)
    column = lax.axis_index("col")
    columns = lax.axis_size("col")
    group = HEADS // KV_HEADS
    head_block = HEADS // columns
    feature_block = head_block * HD
    inv_root = 1.0 / math.sqrt(HD)
    rows_here, span, kv_width = key_cache.shape
    total_rows = residual.shape[1]
    width_share = residual.shape[2]
    hidden_share = gate_weight.shape[1]
    positions = column * span + lax.iota(jnp.int32, span)
    live = positions[None, :] < lengths[:, None]
    cached_keys = key_cache.reshape(rows_here, span, KV_HEADS, HD)
    cached_values = value_cache.reshape(rows_here, span, KV_HEADS, HD)
    gains = norm_gain.astype(jnp.float32)
    finished = []
    for step in range(2):
        queries = query[step].reshape(rows_here, KV_HEADS, group, HD)

        def local_part():
            return partial_softmax(queries, cached_keys, cached_values, live)

        def empty_part():
            return (
                jnp.full((rows_here, KV_HEADS, group), very_low, jnp.float32),
                jnp.zeros((rows_here, KV_HEADS, group), jnp.float32),
                jnp.zeros((rows_here, KV_HEADS, group, HD), jnp.float32),
            )

        peak, total, summed = lax.cond(serving, local_part, empty_part)
        fresh_keys = new_keys[: step + 1].reshape(step + 1, rows_here, KV_HEADS, HD)
        fresh_values = (
            new_values[: step + 1].reshape(step + 1, rows_here, KV_HEADS, HD).astype(jnp.float32)
        )
        fresh_scores = (
            jnp.einsum("bkgd,tbkd->bkgt", queries, fresh_keys, preferred_element_type=jnp.float32)
            * inv_root
        )
        peak, total, summed = joined((peak, total, summed), "col", combine)
        top = jnp.maximum(peak, jnp.max(fresh_scores, axis=-1))
        rescale = jnp.exp(peak - top)
        fresh_weights = jnp.exp(fresh_scores - top[..., None])
        total = total * rescale + jnp.sum(fresh_weights, axis=-1)
        summed = summed * rescale[..., None] + jnp.einsum(
            "bkgt,tbkd->bkgd", fresh_weights, fresh_values, precision=lax.Precision.HIGHEST
        )
        attended = (summed / total[..., None]).reshape(rows_here, HEADS * HD).astype(jnp.bfloat16)
        piece = lax.dynamic_slice_in_dim(attended, column * feature_block, feature_block, 1)
        arrived = cross(piece)
        part = lax.all_gather(arrived, "row", axis=0, tiled=True)
        partial_value = lax.cond(
            ffn_side,
            lambda: jnp.dot(part, out_weight, preferred_element_type=jnp.float32),
            lambda: jnp.zeros((part.shape[0], width_share), jnp.float32),
        )
        mid = residual[step].astype(jnp.float32) + tile_sum(partial_value)
        lifted = (mid * gains).astype(jnp.bfloat16)

        def lift_products():
            return (
                jnp.dot(lifted, gate_weight, preferred_element_type=jnp.float32),
                jnp.dot(lifted, up_weight, preferred_element_type=jnp.float32),
            )

        def lift_empty():
            return (
                jnp.zeros((total_rows, hidden_share), jnp.float32),
                jnp.zeros((total_rows, hidden_share), jnp.float32),
            )

        gate_part, up_part = lax.cond(ffn_side, lift_products, lift_empty)
        gate, up, squares = lax.psum((gate_part, up_part, jnp.sum(mid * mid, axis=1)), "row")
        inv = lax.rsqrt(squares / D + 1e-05)[:, None]
        act = (jax.nn.silu(gate * inv) * (up * inv)).astype(jnp.bfloat16)
        down_part = lax.cond(
            ffn_side,
            lambda: jnp.dot(act, down_weight, preferred_element_type=jnp.float32),
            lambda: jnp.zeros((total_rows, width_share), jnp.float32),
        )
        result = (mid + tile_sum(down_part)).astype(jnp.bfloat16)
        finished.append(result)
    stacked = jnp.stack(finished)
    returned = cross(stacked)
    stacked = jnp.where(serving, returned, stacked)
    return stacked


def solution(mesh):
    in_specs = (
        P(None, "row", None),
        P(None, "row", None),
        P(None, "row", None),
        P("row", "col", None),
        P("row", "col", None),
        P("row"),
        P(None, None, "row"),
        P("col", "row"),
        P("row"),
        P("row", "col"),
        P("row", "col"),
        P("col", "row"),
    )
    out_specs = P(None, None, "row")
    return jax.shard_map(shards, mesh=mesh, in_specs=in_specs, out_specs=out_specs, check_vma=False)
```

profile of v0, /device:TPU:1, one launch (start us, length us, event | category | flops | bytes accessed | tf_op | source)
XLA Modules:
  0.0 613.2 jit_solution(6145842761887544593)
XLA Ops:
  6.5 0.7 slice.26
  7.2 0.7 copy-done.17
  8.0 1.6 copy.23
  9.6 0.4 copy.24
  10.0 0.3 copy-done.20
  10.3 0.1 fusion.47
  10.4 3.5 conditional.8
  10.4 0.9 fusion.36
  11.4 1.6 fusion.1
  13.0 0.9 fusion.2
  13.9 23.1 %all-gather = f32[32,4,8]{2,1,0:T(4,128)S(1)} all-gather(f32[2,4,8]{2,1,0:T(4,128)} %get-tuple-element.449), channel_id=2, replica_groups=mesh['side'=2,'row'=16,'col'=16] {'col'}, dimensions={0}, use_global_device_ids=true | all-gather | bytes 4352 | tf_op jit(solution)/shard_map/all_gather | solution.py:24
  37.0 18.0 %all-gather.1 = f32[32,4,8]{2,1,0:T(4,128)S(1)} all-gather(f32[2,4,8]{2,1,0:T(4,128)S(1)} %get-tuple-element.450), channel_id=3, replica_groups=mesh['side'=2,'row'=16,'col'=16] {'col'}, dimensions={0}, use_global_device_ids=true | all-gather | bytes 4352 | tf_op jit(solution)/shard_map/all_gather | solution.py:24
  55.0 17.7 %all-gather.2 = f32[32,4,8,128]{3,2,1,0:T(8,128)S(1)} all-gather(f32[2,4,8,128]{3,2,1,0:T(8,128)S(1)} %get-tuple-element.451), channel_id=4, replica_groups=mesh['side'=2,'row'=16,'col'=16] {'col'}, dimensions={0}, use_global_device_ids=true | all-gather | bytes 557056 | tf_op jit(solution)/shard_map/all_gather | solution.py:24
  72.7 2.1 while.38
  72.8 0.1 fusion.77
  73.0 0.1 fusion.77
  73.1 0.1 fusion.77
  73.3 0.1 fusion.77
  73.4 0.1 fusion.77
  73.6 0.1 fusion.77
  73.7 0.1 fusion.77
  73.8 0.1 fusion.77
  74.0 0.1 fusion.77
  74.1 0.1 fusion.77
  74.3 0.1 fusion.77
  74.4 0.1 fusion.77
  74.8 0.1 fusion.25
  75.0 1.9 collective-permute-start
  76.9 0.1 fusion.38
  77.1 3.5 conditional.12
  77.1 0.9 fusion.37
  78.0 1.6 fusion.11
  79.7 0.9 fusion.12
  80.5 18.0 %all-gather.3 = f32[32,4,8]{2,1,0:T(4,128)S(1)} all-gather(f32[2,4,8]{2,1,0:T(4,128)} %get-tuple-element.457), channel_id=5, replica_groups=mesh['side'=2,'row'=16,'col'=16] {'col'}, dimensions={0}, use_global_device_ids=true | all-gather | bytes 4352 | tf_op jit(solution)/shard_map/all_gather | solution.py:24
  98.6 16.4 %all-gather.4 = f32[32,4,8]{2,1,0:T(4,128)S(1)} all-gather(f32[2,4,8]{2,1,0:T(4,128)S(1)} %get-tuple-element.458), channel_id=6, replica_groups=mesh['side'=2,'row'=16,'col'=16] {'col'}, dimensions={0}, use_global_device_ids=true | all-gather | bytes 4352 | tf_op jit(solution)/shard_map/all_gather | solution.py:24
  115.0 19.1 %all-gather.5 = f32[32,4,8,128]{3,2,1,0:T(8,128)S(1)} all-gather(f32[2,4,8,128]{3,2,1,0:T(8,128)S(1)} %get-tuple-element.459), channel_id=7, replica_groups=mesh['side'=2,'row'=16,'col'=16] {'col'}, dimensions={0}, use_global_device_ids=true | all-gather | bytes 557056 | tf_op jit(solution)/shard_map/all_gather | solution.py:24
  134.1 2.1 while.39
  134.2 0.1 fusion.79
  134.3 0.1 fusion.79
  134.8 0.1 fusion.79
  134.9 0.1 fusion.79
  135.3 0.1 fusion.79
  135.9 0.1 fusion.79
  136.4 0.2 fusion.22
  136.6 2.9 collective-permute-start.1
  139.5 25.2 %all-gather.6 = bf16[16,2,256]{2,1,0:T(2,128)(2,1)S(1)} all-gather(bf16[1,2,256]{2,1,0:T(2,128)(2,1)S(1)} %bitcast.148), channel_id=1, replica_groups=mesh['side'=2,'row'=16,'col'=16] {'row'}, dimensions={0}, use_global_device_ids=true | all-gather | bytes 17408 | tf_op jit(solution)/shard_map/all_gather | solution.py:134
  164.7 19.0 %all-gather.7 = bf16[16,2,256]{2,1,0:T(2,128)(2,1)S(1)} all-gather(bf16[1,2,256]{2,1,0:T(2,128)(2,1)S(1)} %bitcast.149), channel_id=1, replica_groups=mesh['side'=2,'row'=16,'col'=16] {'row'}, dimensions={0}, use_global_device_ids=true | all-gather | bytes 17408 | tf_op jit(solution)/shard_map/all_gather | solution.py:134
  183.7 0.6 copy-done.9
  184.4 0.6 copy-done.10
  185.1 140.0 %all-reduce.10.cloned.1.call-done = (f32[32,512]{1,0:T(8,128)}, f32[32,512]{1,0:T(8,128)}) async-done(((f32[32,512]{1,0:T(8,128)}, f32[32,512]{1,0:T(8,128)}), (f32[32,512]{1,0:T(8,128)}, f32[32,512]{1,0:T(8,128)})) %all-reduce.10.cloned.1.call-update) | async-done | bytes 131088 | tf_op jit(solution)/shard_map/psum | solution.py:52
  325.1 1.0 multiply_reduce_fusion.1
  326.2 0.6 copy-done.5
  327.0 0.6 copy-done.7
  327.7 24.6 %all-reduce.2 = (f32[32]{0:T(128)S(1)}, f32[32]{0:T(128)S(1)}) all-reduce(f32[32]{0:T(128)S(1)} %get-tuple-element.484, f32[32]{0:T(128)S(1)} %get-tuple-element.483), channel_id=1, replica_groups=mesh['side'=2,'row'=16,'col'=16] {'row'}, use_global_device_ids=true, to_apply=%region_33.34 | all-reduce | flops 64 | bytes 512 | tf_op jit(solution)/shard_map/psum | solution.py:156
  352.3 105.3 %all-reduce.12.cloned.1.call-done = (f32[32,896]{1,0:T(8,128)}, f32[32,896]{1,0:T(8,128)}, f32[32,896]{1,0:T(8,128)}, f32[32,896]{1,0:T(8,128)}) async-done(((f32[32,896]{1,0:T(8,128)}, f32[32,896]{1,0:T(8,128)}, f32[32,896]{1,0:T(8,128)}, f32[32,896]{1,0:T(8,128)}), (f32[32,896]{1,0:T(8,128)}, f32[32,896]{1,0:T(8,128)}, f32[32,896]{1,0:T(8,128)}, f32[32,896]{1,0:T(8,128)})) %all-reduce.12.cloned.1.call-update) | async-done | bytes 458768 | tf_op jit(solution)/shard_map/psum | solution.py:156
  457.6 1.1 multiply_convert_fusion
  458.7 1.1 multiply_convert_fusion.1
  459.8 0.6 copy-done.11
  460.5 0.6 copy-done.12
  461.1 137.5 %all-reduce.8.cloned.1.call-done = (f32[32,512]{1,0:T(8,128)}, f32[32,512]{1,0:T(8,128)}) async-done(((f32[32,512]{1,0:T(8,128)}, f32[32,512]{1,0:T(8,128)}), (f32[32,512]{1,0:T(8,128)}, f32[32,512]{1,0:T(8,128)})) %all-reduce.8.cloned.1.call-update) | async-done | bytes 131088 | tf_op jit(solution)/shard_map/psum | solution.py:52
  598.6 0.9 fusion.23
  599.5 4.3 collective-permute-start.2
  603.8 2.2 collective-permute-done.2
  606.0 0.6 broadcast_select_fusion
  (125 shorter events, 2.7 us)
Async XLA Ops:
  6.5 1.4 copy-start.16
  6.5 318.6 %all-reduce.10.cloned.1.call-start = ((), (), s32[]{:S(2)}) async-start(), calls=%async_computation.1 | async-start | bytes 262144 | tf_op jit(solution)/shard_map/psum | solution.py:52
  7.2 0.7 copy-start.17
  8.0 1.6 copy-start.4
  9.6 0.7 copy-start.20
  74.9 2.0 copy-start.18
  75.0 64.6 %collective-permute-start = (bf16[2,256]{1,0:T(2,128)(2,1)S(1)}, bf16[2,256]{1,0:T(2,128)(2,1)S(1)}, u32[]{:S(2)}, u32[]{:S(2)}) collective-permute-start(bf16[2,256]{1,0:T(2,128)(2,1)S(1)} %constant_dynamic-slice_fusion.1), channel_id=1, source_target_pairs={{0,256},{256,0},{1,257},{257,1},{2,258},{258,2},{3,259},{259,3},{4... | collective-permute-start | bytes 3080 | tf_op jit(solution)/shard_map/ppermute | solution.py:20
  115.0 68.7 %copy-start.3 = (bf16[256,512]{1,0:T(8,128)(2,1)S(1)}, bf16[256,512]{1,0:T(8,128)(2,1)}, u32[]{:S(2)}) copy-start(bf16[256,512]{1,0:T(8,128)(2,1)} %param.39) | copy-start | bytes 786436
  134.1 50.9 %copy-start.19 = (bf16[512]{0:T(512)(128)(2,1)S(1)}, bf16[512]{0:T(512)(128)(2,1)}, u32[]{:S(2)}) copy-start(bf16[512]{0:T(512)(128)(2,1)} %param.40) | copy-start | bytes 3076
  134.1 191.0 %copy-start.13 = (bf16[2,32,512]{2,1,0:T(8,128)(2,1)S(1)}, bf16[2,32,512]{2,1,0:T(8,128)(2,1)}, u32[]{:S(2)}) copy-start(bf16[2,32,512]{2,1,0:T(8,128)(2,1)} %param.38) | copy-start | bytes 196612
  134.1 192.0 %copy-start.1 = (bf16[512,896]{1,0:T(8,128)(2,1)S(1)}, bf16[512,896]{1,0:T(8,128)(2,1)}, u32[]{:S(2)}) copy-start(bf16[512,896]{1,0:T(8,128)(2,1)} %param.42) | copy-start | bytes 2752516
  136.3 189.9 %copy-start = (bf16[512,896]{1,0:T(8,128)(2,1)S(1)}, bf16[512,896]{1,0:T(8,128)(2,1)}, u32[]{:S(2)}) copy-start(bf16[512,896]{1,0:T(8,128)(2,1)} %param.41) | copy-start | bytes 2752516
  136.6 28.1 %collective-permute-start.1 = (bf16[2,256]{1,0:T(2,128)(2,1)S(1)}, bf16[2,256]{1,0:T(2,128)(2,1)S(1)}, u32[]{:S(2)}, u32[]{:S(2)}) collective-permute-start(bf16[2,256]{1,0:T(2,128)(2,1)S(1)} %constant_dynamic-slice_fusion), channel_id=1, source_target_pairs={{0,256},{256,0},{1,257},{257,1},{2,258},{258,2},{3,259},{259,3},{4... | collective-permute-start | bytes 3080 | tf_op jit(solution)/shard_map/ppermute | solution.py:20
  183.7 0.6 copy-start.9
  184.4 0.6 copy-start.10
  185.0 272.6 %all-reduce.12.cloned.1.call-start = ((), (), s32[]{:S(2)}) async-start(), calls=%async_computation.2 | async-start | bytes 917504 | tf_op jit(solution)/shard_map/psum | solution.py:156
  326.2 0.6 copy-start.5
  326.2 0.7 copy-start.6
  326.9 0.7 copy-start.7
  326.9 0.7 copy-start.8
  326.9 132.8 %copy-start.2 = (bf16[896,512]{1,0:T(8,128)(2,1)S(1)}, bf16[896,512]{1,0:T(8,128)(2,1)}, u32[]{:S(2)}) copy-start(bf16[896,512]{1,0:T(8,128)(2,1)} %param.43) | copy-start | bytes 2752516
  327.6 270.9 %all-reduce.8.cloned.1.call-start = ((), (), s32[]{:S(2)}) async-start(), calls=%async_computation | async-start | bytes 262144 | tf_op jit(solution)/shard_map/psum | solution.py:52
  459.8 0.6 copy-start.11
  460.4 0.6 copy-start.12
  460.4 138.2 %copy-start.14 = (f32[32,512]{1,0:T(8,128)S(1)}, f32[32,512]{1,0:T(8,128)}, u32[]{:S(2)}) copy-start(f32[32,512]{1,0:T(8,128)} %get-tuple-element.515) | copy-start | bytes 196612
  460.5 138.2 %copy-start.15 = (f32[32,512]{1,0:T(8,128)S(1)}, f32[32,512]{1,0:T(8,128)}, u32[]{:S(2)}) copy-start(f32[32,512]{1,0:T(8,128)} %get-tuple-element.516) | copy-start | bytes 196612
  599.5 6.5 %collective-permute-start.2 = (bf16[2,32,512]{2,1,0:T(8,128)(2,1)S(1)}, bf16[2,32,512]{2,1,0:T(8,128)(2,1)S(1)}, u32[]{:S(2)}, u32[]{:S(2)}) collective-permute-start(bf16[2,32,512]{2,1,0:T(8,128)(2,1)S(1)} %pad_maximum_fusion), channel_id=1, source_target_pairs={{0,256},{256,0},{1,257},{257,1},{2,258},{258,2},{3,259},{259,3},{4... | collective-permute-start | bytes 196616 | tf_op jit(solution)/shard_map/ppermute | solution.py:20
Sparse Core Ops, SparseCore 0:
  185.1 139.9 all-reduce.9
  327.9 129.6 all-reduce.11
  461.2 137.3 all-reduce.7
where the time goes:
time: 614 us; the launch traced here: 613 us
  waiting for transfers between devices  385 us (63%)
  blocking collectives  181 us (29%)
  between operations  13.5 us (2%)
  other arithmetic  10.2 us (2%)
  starting transfers between devices  9.19 us (1%)
  local copies, waits for them, and re-layouts  7.64 us (1%)
    psum x2, waiting for transfers between devices, tile_sum(): return lax.psum(value, 'col')  278 us
    all_gather x6, blocking collectives, joined(): gathered = jax.tree.map(lambda a: lax.all_gather(a, axis), part)  112 us
    psum x1, waiting for transfers between devices, shards(): lax.psum((gate_part, up_part, jnp.sum(mid * mid, axis=1)), 'row')  105 us
    all_gather x2, blocking collectives, shards(): part = lax.all_gather(arrived, 'row', axis=0, tiled=True)  44.2 us
    psum x1, blocking collectives, shards(): lax.psum((gate_part, up_part, jnp.sum(mid * mid, axis=1)), 'row')  24.6 us
  transfers between devices with their start and end apart: 6, of which 4 were waited for; matrix products, arithmetic and copies ran while one was open for 1% of the time, Pallas kernels for 0%

commit v1 on v0

v1 whole, which is shorter than its diff:
```python
import functools
import math

import jax
import jax.numpy as jnp
from jax import lax
from jax.experimental import pallas as pl
from jax.experimental.pallas import tpu as pltpu
from jax.sharding import PartitionSpec as P

D = 8192
KV = 4
HD = 128
N = 16
SPAN = 384
VERY_LOW = -1e30
F32 = jnp.float32
BF16 = jnp.bfloat16
MESH = pl.DeviceIdType.MESH


def kernel(
    len_ref, q_hbm, nk_hbm, nv_hbm, k_hbm, v_hbm, res_hbm, ow_hbm, gain_hbm, gw_hbm, uw_hbm, dw_hbm,
    out_ref,
    q_v, nk_v, nv_v, k_v, v_v, res_v, ow_v, gain_v, gw_v, uw_v, dw_v,
    qbd, heads, resp,
    st_a, rc_a, st_b, rc_b, st_c, rc_c, st_d, rc_d, st_e32, st_e, rc_e, st_f, rc_f, f32f, st_g, rc_g, st_h,
    load_sem, send_sem, recv_sem,
):
    s = lax.axis_index("side")
    r = lax.axis_index("row")
    c = lax.axis_index("col")

    loads = [
        pltpu.make_async_copy(src, dst, load_sem.at[i])
        for i, (src, dst) in enumerate(
            [
                (q_hbm, q_v),
                (k_hbm.at[s], k_v),
                (v_hbm.at[s], v_v),
                (nk_hbm, nk_v),
                (nv_hbm, nv_v),
                (res_hbm, res_v),
                (gain_hbm, gain_v),
                (ow_hbm, ow_v),
                (gw_hbm, gw_v),
                (uw_hbm, uw_v),
                (dw_hbm, dw_v),
            ]
        )
    ]
    for copy in loads:
        copy.start()

    barrier = pltpu.get_barrier_semaphore()

    def greet_row(i, _):
        pl.semaphore_signal(barrier, inc=1, device_id=(s, lax.rem(r + i, N), c), device_id_type=MESH)
        return 0

    def greet_col(i, _):
        other = lax.rem(s * N + c + i, 2 * N)
        pl.semaphore_signal(
            barrier, inc=1, device_id=(other // N, r, lax.rem(other, N)), device_id_type=MESH
        )
        return 0

    lax.fori_loop(1, N, greet_row, 0)
    lax.fori_loop(1, 2 * N, greet_col, 0)

    def exchange(phase, source, target, peer_id):
        def one(i, _):
            peer = peer_id(i)
            pltpu.make_async_remote_copy(
                src_ref=source(peer),
                dst_ref=target,
                send_sem=send_sem.at[phase],
                recv_sem=recv_sem.at[phase],
                device_id=(s, r, peer) if phase in COL_PHASES else (s, peer, c),
                device_id_type=MESH,
            ).start()
            return 0

        lax.fori_loop(1, N, one, 0)

    COL_PHASES = (0, 2, 3, 6)

    def col_peer(i):
        return lax.rem(c + i, N)

    def row_peer(i):
        return lax.rem(r + i, N)

    def rows_at(ref, at, rows):
        return ref.at[pl.ds(pl.multiple_of(at * rows, rows), rows)]

    def arrived(phase, ref):
        pltpu.make_async_copy(ref, ref, recv_sem.at[phase]).wait()

    qbd[...] = jnp.zeros_like(qbd)
    loads[0].wait()
    query = q_v[...].astype(F32)
    for t in range(2):
        mine = jnp.where(s == 0, query[t, 0:1, :], query[t, 1:2, :])
        for h in range(KV * 8):
            g = h // 8
            one_head = mine[:, h * HD : (h + 1) * HD]
            qbd[2 * h + t : 2 * h + t + 1, g * HD : (g + 1) * HD] = one_head
            heads[h // 2, 2 * (h % 2) + t : 2 * (h % 2) + t + 1, :] = one_head
    loads[1].wait()
    scale = 1.0 / math.sqrt(HD)
    scores = (
        lax.dot_general(
            qbd[...].astype(BF16), k_v[...], (((1,), (1,)), ((), ())), preferred_element_type=F32
        )
        * scale
    )
    live = c * SPAN + lax.broadcasted_iota(jnp.int32, scores.shape, 1) < len_ref[s]
    scores = jnp.where(live, scores, VERY_LOW)
    peak = jnp.max(scores, axis=1, keepdims=True)
    weights = jnp.where(live, jnp.exp(scores - peak), 0.0)
    total = jnp.sum(weights, axis=1, keepdims=True)
    loads[2].wait()
    summed = jnp.dot(weights.astype(BF16), v_v[...], preferred_element_type=F32)
    low_lane = lax.broadcasted_iota(jnp.int32, (64, HD), 1) < HD // 2
    stats = jnp.where(low_lane, peak, total)
    for o in range(N):
        g = o // 4
        st_a[8 * o : 8 * o + 4, :] = summed[4 * o : 4 * o + 4, g * HD : (g + 1) * HD]
        st_a[8 * o + 4 : 8 * o + 8, :] = stats[4 * o : 4 * o + 4, :]

    pl.semaphore_wait(barrier, 3 * N - 2)
    exchange(0, lambda peer: rows_at(st_a, peer, 8), rows_at(rc_a, c, 8), col_peer)
    rows_at(rc_a, c, 8)[...] = rows_at(st_a, c, 8)[...]

    group_lanes = pl.ds(pl.multiple_of((c // 4) * HD, HD), HD)
    for copy in loads[3:8]:
        copy.wait()
    q4 = heads[c]
    fresh_k = nk_v[:, :, group_lanes].astype(F32)
    fresh_v = nv_v[:, :, group_lanes].astype(F32)
    nk = [jnp.where(s == 0, fresh_k[t, 0:1, :], fresh_k[t, 1:2, :]) for t in range(2)]
    nv = [jnp.where(s == 0, fresh_v[t, 0:1, :], fresh_v[t, 1:2, :]) for t in range(2)]
    second = lax.rem(lax.broadcasted_iota(jnp.int32, (4, HD), 0), 2) == 1
    f0 = jnp.broadcast_to(jnp.sum(q4 * nk[0], axis=1, keepdims=True) * scale, (4, HD))
    f1 = jnp.broadcast_to(jnp.sum(q4 * nk[1], axis=1, keepdims=True) * scale, (4, HD))
    f1 = jnp.where(second, f1, VERY_LOW)
    own_row = lax.broadcasted_iota(jnp.int32, (2 * N, 512), 0) == 2 * c + s
    for t in range(2):
        row = jnp.sum(jnp.where(own_row, res_v[t].astype(F32), 0.0), axis=0, keepdims=True)
        for k in range(4):
            resp[2 * k + t : 2 * k + t + 1, :] = row[:, k * HD : (k + 1) * HD]
    gains = gain_v[...].astype(F32).reshape(1, 512)

    arrived(0, rc_a.at[pl.ds(0, 8 * (N - 1))])
    blocks = rc_a[...].reshape(N, 8, HD)
    sums, stat = blocks[:, 0:4, :], blocks[:, 4:8, :]
    low = lax.broadcasted_iota(jnp.int32, (N, 4, HD), 2) < HD // 2
    turned = pltpu.roll(stat, HD // 2, 2)
    peaks = jnp.where(low, stat, turned)
    totals = jnp.where(low, turned, stat)
    top = jnp.maximum(jnp.max(peaks, axis=0), jnp.maximum(f0, f1))
    share = jnp.exp(peaks - top[None])
    e0 = jnp.exp(f0 - top)
    e1 = jnp.where(second, jnp.exp(f1 - top), 0.0)
    whole = jnp.sum(share * totals, axis=0) + e0 + e1
    mixed = jnp.sum(share * sums, axis=0) + e0 * nv[0] + e1 * nv[1]
    st_b[...] = (mixed / whole).astype(BF16).astype(F32)

    exchange(1, lambda peer: st_b, rc_b.at[r], row_peer)
    rc_b[r] = st_b[...]
    arrived(1, rc_b.at[pl.ds(0, N - 1)])

    def gather(ref, count, stride):
        return jnp.concatenate(
            [
                jnp.concatenate(
                    [ref[pl.ds(2 * k + t, N, stride=stride), :] for k in range(count)], axis=1
                )
                for t in range(2)
            ],
            axis=0,
        )

    def scatter(ref, value, count, stride, base=0):
        for t in range(2):
            for k in range(count):
                ref[pl.ds(base + 2 * k + t, N, stride=stride), :] = value[
                    N * t : N * (t + 1), k * HD : (k + 1) * HD
                ]

    attended = jnp.concatenate(
        [jnp.concatenate([rc_b[:, 2 * j + t, :] for j in range(2)], axis=1) for t in range(2)], axis=0
    )
    part = jnp.dot(attended.astype(BF16), ow_v[...], preferred_element_type=F32)
    scatter(st_c, part, 4, 8)
    exchange(2, lambda peer: rows_at(st_c, peer, 8), rows_at(rc_c, c, 8), col_peer)
    rows_at(rc_c, c, 8)[...] = rows_at(st_c, c, 8)[...]
    arrived(2, rc_c.at[pl.ds(0, 8 * (N - 1))])
    mid_piece = resp[...] + jnp.sum(rc_c[...].reshape(N, 8, HD), axis=0)

    st_d[...] = mid_piece
    exchange(3, lambda peer: st_d, rows_at(rc_d, c, 8), col_peer)
    rows_at(rc_d, c, 8)[...] = st_d[...]
    arrived(3, rc_d.at[pl.ds(0, 8 * (N - 1))])
    mid = gather(rc_d, 4, 8)
    lifted = (mid * gains).astype(BF16)
    squares = jnp.broadcast_to(jnp.sum(mid * mid, axis=1, keepdims=True), (2 * N, HD))
    squares_high = squares.astype(BF16).astype(F32)
    scatter(st_e32, squares_high, 1, 32, 14)
    scatter(st_e32, squares - squares_high, 1, 32, 30)
    loads[8].wait()
    scatter(st_e32, jnp.dot(lifted, gw_v[...], preferred_element_type=F32), 7, 32)
    loads[9].wait()
    scatter(st_e32, jnp.dot(lifted, uw_v[...], preferred_element_type=F32), 7, 32, 16)
    st_e[...] = st_e32[...].astype(BF16)
    exchange(4, lambda peer: rows_at(st_e, peer, 32), rows_at(rc_e, r, 32), row_peer)
    rows_at(rc_e, r, 32)[...] = rows_at(st_e, r, 32)[...]
    arrived(4, rc_e.at[pl.ds(0, 32 * (N - 1))])
    lifts = jnp.sum(rc_e[...].astype(F32).reshape(N, 32, HD), axis=0)
    gate, up = lifts[0:16], lifts[16:32]
    inv0 = lax.rsqrt((gate[14:15] + up[14:15]) / D + 1e-05)
    inv1 = lax.rsqrt((gate[15:16] + up[15:16]) / D + 1e-05)
    odd = lax.rem(lax.broadcasted_iota(jnp.int32, (16, HD), 0), 2) == 1
    inv = jnp.where(odd, inv1, inv0)
    gate, up = gate * inv, up * inv
    st_f[...] = (gate / (1.0 + jnp.exp(-gate)) * up).astype(BF16)

    exchange(5, lambda peer: st_f, rows_at(rc_f, r, 16), row_peer)
    rows_at(rc_f, r, 16)[...] = st_f[...]
    loads[10].wait()
    arrived(5, rc_f.at[pl.ds(0, 16 * (N - 1))])
    f32f[...] = rc_f[...].astype(F32)
    act = gather(f32f, 7, 16).astype(BF16)
    scatter(st_g, jnp.dot(act, dw_v[...], preferred_element_type=F32), 4, 8)
    exchange(6, lambda peer: rows_at(st_g, peer, 8), rows_at(rc_g, c, 8), col_peer)
    rows_at(rc_g, c, 8)[...] = rows_at(st_g, c, 8)[...]
    arrived(6, rc_g.at[pl.ds(0, 8 * (N - 1))])
    st_h[...] = (st_d[...] + jnp.sum(rc_g[...].reshape(N, 8, HD), axis=0)).astype(BF16)

    here = s * N + c

    def give(i, _):
        other = lax.rem(here + i, 2 * N)
        pltpu.make_async_remote_copy(
            src_ref=st_h,
            dst_ref=out_ref.at[here],
            send_sem=send_sem.at[7],
            recv_sem=recv_sem.at[7],
            device_id=(other // N, r, lax.rem(other, N)),
            device_id_type=MESH,
        ).start()
        return 0

    lax.fori_loop(1, 2 * N, give, 0)
    out_ref[here] = st_h[...]

    def sent(phase, ref):
        pltpu.make_async_copy(ref, ref, send_sem.at[phase]).wait()

    sent(0, rc_a.at[pl.ds(0, 8 * (N - 1))])
    sent(1, rc_b.at[pl.ds(0, N - 1)])
    sent(2, rc_c.at[pl.ds(0, 8 * (N - 1))])
    sent(3, rc_d.at[pl.ds(0, 8 * (N - 1))])
    sent(4, rc_e.at[pl.ds(0, 32 * (N - 1))])
    sent(5, rc_f.at[pl.ds(0, 16 * (N - 1))])
    sent(6, rc_g.at[pl.ds(0, 8 * (N - 1))])
    arrived(7, out_ref.at[pl.ds(0, 2 * N - 1)])
    sent(7, out_ref.at[pl.ds(0, 2 * N - 1)])


def shards(query, new_keys, new_values, key_cache, value_cache, lengths, residual, out_weight,
           norm_gain, gate_weight, up_weight, down_weight):
    def vm(*shape, kind=F32):
        return pltpu.VMEM(shape, kind)

    hbm = pl.BlockSpec(memory_space=pl.ANY)
    pieces = pl.pallas_call(
        kernel,
        out_shape=jax.ShapeDtypeStruct((2 * N, 8, HD), BF16),
        in_specs=[pl.BlockSpec(memory_space=pltpu.SMEM)] + [hbm] * 11,
        out_specs=pl.BlockSpec(memory_space=pltpu.VMEM),
        scratch_shapes=[
            vm(2, 2, 4096, kind=BF16),
            vm(2, 2, 512, kind=BF16),
            vm(2, 2, 512, kind=BF16),
            vm(SPAN, 512, kind=BF16),
            vm(SPAN, 512, kind=BF16),
            vm(2, 32, 512, kind=BF16),
            vm(256, 512, kind=BF16),
            vm(512, kind=BF16),
            vm(512, 896, kind=BF16),
            vm(512, 896, kind=BF16),
            vm(896, 512, kind=BF16),
            vm(64, 512),
            vm(N, 4, HD),
            vm(8, HD),
            vm(8 * N, HD), vm(8 * N, HD),
            vm(4, HD), vm(N, 4, HD),
            vm(8 * N, HD), vm(8 * N, HD),
            vm(8, HD), vm(8 * N, HD),
            vm(32 * N, HD), vm(32 * N, HD, kind=BF16), vm(32 * N, HD, kind=BF16),
            vm(16, HD, kind=BF16), vm(16 * N, HD, kind=BF16), vm(16 * N, HD),
            vm(8 * N, HD), vm(8 * N, HD),
            vm(8, HD, kind=BF16),
            pltpu.SemaphoreType.DMA((11,)),
            pltpu.SemaphoreType.DMA((8,)),
            pltpu.SemaphoreType.DMA((8,)),
        ],
        compiler_params=pltpu.CompilerParams(
            collective_id=0, has_side_effects=True, vmem_limit_bytes=40 * 1024 * 1024
        ),
        name="layer",
    )(lengths, query, new_keys, new_values, key_cache, value_cache, residual, out_weight, norm_gain,
      gate_weight, up_weight, down_weight)
    pieces = pieces.reshape(2, N, 4, 2, HD)
    return pieces.transpose(3, 1, 0, 2, 4).reshape(2, 2 * N, 512)


def solution(mesh):
    in_specs = (
        P(None, "row", None),
        P(None, "row", None),
        P(None, "row", None),
        P("row", "col", None),
        P("row", "col", None),
        P("row"),
        P(None, None, "row"),
        P("col", "row"),
        P("row"),
        P("row", "col"),
        P("row", "col"),
        P("col", "row"),
    )
    out_specs = P(None, None, "row")
    return jax.shard_map(shards, mesh=mesh, in_specs=in_specs, out_specs=out_specs, check_vma=False)
```

time: 614 us -> 77.5 us (0.13)
  waiting for transfers between devices: 385 us -> 0 us
  blocking collectives: 181 us -> 0 us
  Pallas kernels: 0 us -> 65.2 us
  between operations: 13.5 us -> 0.03 us
  other arithmetic: 10.2 us -> 0 us
  starting transfers between devices: 9.19 us -> 0 us
    psum x3 -> x0, waiting for transfers between devices: 383 us -> none  [the longest x2 278 us: tile_sum(): return lax.psum(value, 'col')]
    all_gather x8 -> x0, blocking collectives: 157 us -> none  [the longest x6 112 us: joined(): gathered = jax.tree.map(lambda a: lax.all_gather(a, axis), part)]
    pallas_call x0 -> x1, Pallas kernels: none -> 65.2 us  [shards(): pl.pallas_call(kernel, out_shape=jax.ShapeDtypeStruct((2 * N, 8, HD), BF1...]
    psum x1 -> x0, blocking collectives: 24.6 us -> none  [shards(): lax.psum((gate_part, up_part, jnp.sum(mid * mid, axis=1)), 'row')]
    ppermute x3 -> x0, starting transfers between devices: 9.1 us -> none  [partner(): return lax.ppermute(value, axis, pairs)]
  transfers between devices with their start and end apart: 6 -> 0, of which waited for: 4 -> 0; matrix products, arithmetic and copies ran while one was open for 1% -> 0% of each run, Pallas kernels for 0% -> 0%
where the time goes in v1:
time: 77.5 us; the launch traced here: 77 us
  Pallas kernels  65.2 us (84%)
  local copies, waits for them, and re-layouts  11.7 us (15%)
    pallas_call x1, Pallas kernels, shards(): pl.pallas_call(kernel, out_shape=jax.ShapeDtypeStruct((2 * N, 8, HD), BF1...  65.2 us
    unnamed x24, local copies, waits for them, and re-layouts  11.1 us

profile of v1, /device:TPU:1, one launch (start us, length us, event | category | flops | bytes accessed | tf_op | source)
XLA Modules:
  0.0 77.0 jit_solution(18139573980013007861)
XLA Ops:
  0.0 0.0 copy-start
  0.0 1.2 %copy-done = bf16[512,896]{1,0:T(8,128)(2,1)S(1)} copy-done((bf16[512,896]{1,0:T(8,128)(2,1)S(1)}, bf16[512,896]{1,0:T(8,128)(2,1)}, u32[]{:S(2)}) %copy-start) | copy-done | bytes 917528
  1.2 0.0 copy-start.1
  1.2 1.2 %copy-done.1 = bf16[512,896]{1,0:T(8,128)(2,1)S(1)} copy-done((bf16[512,896]{1,0:T(8,128)(2,1)S(1)}, bf16[512,896]{1,0:T(8,128)(2,1)}, u32[]{:S(2)}) %copy-start.1) | copy-done | bytes 917528
  2.4 0.0 copy-start.2
  2.4 1.2 %copy-done.2 = bf16[896,512]{1,0:T(8,128)(2,1)S(1)} copy-done((bf16[896,512]{1,0:T(8,128)(2,1)S(1)}, bf16[896,512]{1,0:T(8,128)(2,1)}, u32[]{:S(2)}) %copy-start.2) | copy-done | bytes 917528
  3.5 0.0 copy-start.3
  3.5 1.1 %copy-done.3 = bf16[2,384,512]{2,1,0:T(8,128)(2,1)S(1)} copy-done((bf16[2,384,512]{2,1,0:T(8,128)(2,1)S(1)}, bf16[2,384,512]{2,1,0:T(8,128)(2,1)}, u32[]{:S(2)}) %copy-start.3) | copy-done | bytes 786456
  4.7 0.0 copy-start.4
  4.7 1.1 %copy-done.4 = bf16[2,384,512]{2,1,0:T(8,128)(2,1)S(1)} copy-done((bf16[2,384,512]{2,1,0:T(8,128)(2,1)S(1)}, bf16[2,384,512]{2,1,0:T(8,128)(2,1)}, u32[]{:S(2)}) %copy-start.4) | copy-done | bytes 786456
  5.8 0.0 copy-start.5
  5.8 0.9 %copy-done.5 = bf16[256,512]{1,0:T(8,128)(2,1)S(1)} copy-done((bf16[256,512]{1,0:T(8,128)(2,1)S(1)}, bf16[256,512]{1,0:T(8,128)(2,1)}, u32[]{:S(2)}) %copy-start.5) | copy-done | bytes 262168
  6.8 0.0 copy-start.6
  6.8 0.8 %copy-done.6 = bf16[2,32,512]{2,1,0:T(8,128)(2,1)S(1)} copy-done((bf16[2,32,512]{2,1,0:T(8,128)(2,1)S(1)}, bf16[2,32,512]{2,1,0:T(8,128)(2,1)}, u32[]{:S(2)}) %copy-start.6) | copy-done | bytes 65560
  7.6 0.0 copy-start.7
  7.6 0.8 copy-done.7
  8.4 0.0 copy-start.8
  8.4 0.7 copy-done.8
  9.0 0.0 copy-start.9
  9.0 0.7 copy-done.9
  9.7 0.0 copy-start.10
  9.7 0.7 copy-done.10
  10.4 0.0 copy-start.11
  10.4 0.7 copy-done.11
  11.1 65.2 %layer.1 = bf16[32,8,128]{2,1,0:T(8,128)(2,1)S(1)} custom-call(s32[2]{0:T(128)S(1)} %copy-done.11, bf16[2,2,4096]{2,1,0:T(2,128)(2,1)S(1)} %copy-done.7, bf16[2,2,512]{2,1,0:T(2,128)(2,1)S(1)} %copy-done.8, bf16[2,2,512]{2,1,0:T(2,128)(2,1)S(1)} %copy-done.9, bf16[2,384,512]{2,1,0:T(8,128)(2,1)S(1)} %copy-done.3, bf16[2,384,512]{2,1,0:T(8,128)(2,1)S(1)} %copy-done.4, ...), custom_call_target="tpu_custom_call" | custom-call | tf_op jit(solution)/shard_map/layer/pallas_call | solution.py:278
  76.3 0.7 reshape.7
  (1 shorter events, 0.0 us)
Async XLA Ops:
  0.0 1.2 %copy-start = (bf16[512,896]{1,0:T(8,128)(2,1)S(1)}, bf16[512,896]{1,0:T(8,128)(2,1)}, u32[]{:S(2)}) copy-start(bf16[512,896]{1,0:T(8,128)(2,1)} %gw_hbm.1) | copy-start | bytes 2752516
  1.2 1.2 %copy-start.1 = (bf16[512,896]{1,0:T(8,128)(2,1)S(1)}, bf16[512,896]{1,0:T(8,128)(2,1)}, u32[]{:S(2)}) copy-start(bf16[512,896]{1,0:T(8,128)(2,1)} %uw_hbm.1) | copy-start | bytes 2752516
  2.4 1.2 %copy-start.2 = (bf16[896,512]{1,0:T(8,128)(2,1)S(1)}, bf16[896,512]{1,0:T(8,128)(2,1)}, u32[]{:S(2)}) copy-start(bf16[896,512]{1,0:T(8,128)(2,1)} %dw_hbm.1) | copy-start | bytes 2752516
  3.5 1.1 %copy-start.3 = (bf16[2,384,512]{2,1,0:T(8,128)(2,1)S(1)}, bf16[2,384,512]{2,1,0:T(8,128)(2,1)}, u32[]{:S(2)}) copy-start(bf16[2,384,512]{2,1,0:T(8,128)(2,1)} %k_hbm.1) | copy-start | bytes 2359300
  4.7 1.1 %copy-start.4 = (bf16[2,384,512]{2,1,0:T(8,128)(2,1)S(1)}, bf16[2,384,512]{2,1,0:T(8,128)(2,1)}, u32[]{:S(2)}) copy-start(bf16[2,384,512]{2,1,0:T(8,128)(2,1)} %v_hbm.1) | copy-start | bytes 2359300
  5.8 0.9 %copy-start.5 = (bf16[256,512]{1,0:T(8,128)(2,1)S(1)}, bf16[256,512]{1,0:T(8,128)(2,1)}, u32[]{:S(2)}) copy-start(bf16[256,512]{1,0:T(8,128)(2,1)} %ow_hbm.1) | copy-start | bytes 786436
  6.8 0.8 %copy-start.6 = (bf16[2,32,512]{2,1,0:T(8,128)(2,1)S(1)}, bf16[2,32,512]{2,1,0:T(8,128)(2,1)}, u32[]{:S(2)}) copy-start(bf16[2,32,512]{2,1,0:T(8,128)(2,1)} %res_hbm.1) | copy-start | bytes 196612
  7.6 0.8 copy-start.7
  8.4 0.7 copy-start.8
  9.0 0.7 copy-start.9
  9.7 0.7 copy-start.10
  10.4 0.7 copy-start.11

commit v2 on v1

--- a/solution.py
+++ b/solution.py
@@ -20,12 +20,12 @@
 
 
 def kernel(
-    len_ref, q_hbm, nk_hbm, nv_hbm, k_hbm, v_hbm, res_hbm, ow_hbm, gain_hbm, gw_hbm, uw_hbm, dw_hbm,
+    len_hbm, q_hbm, nk_hbm, nv_hbm, k_hbm, v_hbm, res_hbm, ow_hbm, gain_hbm, gw_hbm, uw_hbm, dw_hbm,
     out_ref,
-    q_v, nk_v, nv_v, k_v, v_v, res_v, ow_v, gain_v, gw_v, uw_v, dw_v,
+    len_ref, q_v, nk_v, nv_v, k_v, v_v, res_v, ow_v, gain_v, gw_v, uw_v, dw_v,
     qbd, heads, resp,
     st_a, rc_a, st_b, rc_b, st_c, rc_c, st_d, rc_d, st_e32, st_e, rc_e, st_f, rc_f, f32f, st_g, rc_g, st_h,
-    load_sem, send_sem, recv_sem,
+    load_sem, send_sem, recv_sem, met_sem,
 ):
     s = lax.axis_index("side")
     r = lax.axis_index("row")
@@ -46,6 +46,7 @@
                 (gw_hbm, gw_v),
                 (uw_hbm, uw_v),
                 (dw_hbm, dw_v),
+                (len_hbm, len_ref),
             ]
         )
     ]
@@ -54,23 +55,57 @@
 
     barrier = pltpu.get_barrier_semaphore()
 
+    odd = lax.rem(c, 2)
+
     def greet_row(i, _):
-        pl.semaphore_signal(barrier, inc=1, device_id=(s, lax.rem(r + i, N), c), device_id_type=MESH)
+        pl.semaphore_signal(
+            barrier, inc=1, device_id=(s, lax.rem(r + i, N), c - odd + 1), device_id_type=MESH
+        )
         return 0
 
     def greet_col(i, _):
-        other = lax.rem(s * N + c + i, 2 * N)
+        other = lax.rem(s * N + c + odd + i, 2 * N)
         pl.semaphore_signal(
             barrier, inc=1, device_id=(other // N, r, lax.rem(other, N)), device_id_type=MESH
         )
         return 0
 
+    lax.fori_loop(1, N, lambda i, _: greet_col(2 * i, 0), 0)
+
+    @pl.when(odd == 1)
+    def _():
+        greet_col(0, 0)
+
+    @pl.when(odd == 0)
+    def _():
+        pl.semaphore_signal(barrier, inc=1, device_id=(s, r, c + 1), device_id_type=MESH)
+
     lax.fori_loop(1, N, greet_row, 0)
-    lax.fori_loop(1, 2 * N, greet_col, 0)
+
+    def met_columns():
+        @pl.when(odd == 0)
+        def _():
+            pl.semaphore_wait(barrier, 2 * N - 1)
+            pl.semaphore_signal(met_sem, inc=1, device_id=(s, r, c + 1), device_id_type=MESH)
+
+        @pl.when(odd == 1)
+        def _():
+            pl.semaphore_wait(met_sem, 1)
+
+    def met_rows():
+        @pl.when(odd == 1)
+        def _():
+            pl.semaphore_wait(barrier, 2 * N - 1)
+            pl.semaphore_signal(met_sem, inc=1, device_id=(s, r, c - 1), device_id_type=MESH)
+
+        @pl.when(odd == 0)
+        def _():
+            pl.semaphore_wait(met_sem, 1)
 
     def exchange(phase, source, target, peer_id):
         def one(i, _):
-            peer = peer_id(i)
+            half = (i + 1) // 2
+            peer = peer_id(N // 2 + half * (1 - 2 * lax.rem(i, 2)))
             pltpu.make_async_remote_copy(
                 src_ref=source(peer),
                 dst_ref=target,
@@ -81,7 +116,7 @@
             ).start()
             return 0
 
-        lax.fori_loop(1, N, one, 0)
+        lax.fori_loop(0, N - 1, one, 0)
 
     COL_PHASES = (0, 2, 3, 6)
 
@@ -108,6 +143,7 @@
             qbd[2 * h + t : 2 * h + t + 1, g * HD : (g + 1) * HD] = one_head
             heads[h // 2, 2 * (h % 2) + t : 2 * (h % 2) + t + 1, :] = one_head
     loads[1].wait()
+    loads[11].wait()
     scale = 1.0 / math.sqrt(HD)
     scores = (
         lax.dot_general(
@@ -129,7 +165,7 @@
         st_a[8 * o : 8 * o + 4, :] = summed[4 * o : 4 * o + 4, g * HD : (g + 1) * HD]
         st_a[8 * o + 4 : 8 * o + 8, :] = stats[4 * o : 4 * o + 4, :]
 
-    pl.semaphore_wait(barrier, 3 * N - 2)
+    met_columns()
     exchange(0, lambda peer: rows_at(st_a, peer, 8), rows_at(rc_a, c, 8), col_peer)
     rows_at(rc_a, c, 8)[...] = rows_at(st_a, c, 8)[...]
 
@@ -167,6 +203,7 @@
     mixed = jnp.sum(share * sums, axis=0) + e0 * nv[0] + e1 * nv[1]
     st_b[...] = (mixed / whole).astype(BF16).astype(F32)
 
+    met_rows()
     exchange(1, lambda peer: st_b, rc_b.at[r], row_peer)
     rc_b[r] = st_b[...]
     arrived(1, rc_b.at[pl.ds(0, N - 1)])
@@ -274,13 +311,14 @@
     def vm(*shape, kind=F32):
         return pltpu.VMEM(shape, kind)
 
-    hbm = pl.BlockSpec(memory_space=pl.ANY)
+    hbm = pl.BlockSpec(memory_space=pltpu.HBM)
     pieces = pl.pallas_call(
         kernel,
         out_shape=jax.ShapeDtypeStruct((2 * N, 8, HD), BF16),
-        in_specs=[pl.BlockSpec(memory_space=pltpu.SMEM)] + [hbm] * 11,
+        in_specs=[hbm] * 12,
         out_specs=pl.BlockSpec(memory_space=pltpu.VMEM),
         scratch_shapes=[
+            pltpu.SMEM((2,), jnp.int32),
             vm(2, 2, 4096, kind=BF16),
             vm(2, 2, 512, kind=BF16),
             vm(2, 2, 512, kind=BF16),
@@ -303,16 +341,20 @@
             vm(16, HD, kind=BF16), vm(16 * N, HD, kind=BF16), vm(16 * N, HD),
             vm(8 * N, HD), vm(8 * N, HD),
             vm(8, HD, kind=BF16),
-            pltpu.SemaphoreType.DMA((11,)),
+            pltpu.SemaphoreType.DMA((12,)),
             pltpu.SemaphoreType.DMA((8,)),
             pltpu.SemaphoreType.DMA((8,)),
+            pltpu.SemaphoreType.REGULAR,
         ],
         compiler_params=pltpu.CompilerParams(
-            collective_id=0, has_side_effects=True, vmem_limit_bytes=40 * 1024 * 1024
+            collective_id=0, has_side_effects=True, vmem_limit_bytes=32 * 1024 * 1024
         ),
         name="layer",
-    )(lengths, query, new_keys, new_values, key_cache, value_cache, residual, out_weight, norm_gain,
-      gate_weight, up_weight, down_weight)
+    )(*[
+        pltpu.with_memory_space_constraint(a, pltpu.HBM)
+        for a in (lengths, query, new_keys, new_values, key_cache, value_cache, residual, out_weight,
+                  norm_gain, gate_weight, up_weight, down_weight)
+    ])
     pieces = pieces.reshape(2, N, 4, 2, HD)
     return pieces.transpose(3, 1, 0, 2, 4).reshape(2, 2 * N, 512)
 

time: 77.5 us -> 61.7 us (0.80)
  local copies, waits for them, and re-layouts: 11.7 us -> 0.68 us
  Pallas kernels: 65.2 us -> 60.9 us
    unnamed x24 -> x0, local copies, waits for them, and re-layouts: 11.1 us -> none
    pallas_call x1, Pallas kernels: 65.2 us -> 60.9 us  [shards(): pl.pallas_call(kernel, out_shape=jax.ShapeDtypeStruct((2 * N, 8, HD), BF1...]
where the time goes in v2:
time: 61.7 us; the launch traced here: 61.6 us
  Pallas kernels  60.9 us (99%)
  local copies, waits for them, and re-layouts  0.68 us (1%)
    pallas_call x1, Pallas kernels, shards(): pl.pallas_call(kernel, out_shape=jax.ShapeDtypeStruct((2 * N, 8, HD), BF1...  60.9 us

profile of v2, /device:TPU:1, one launch (start us, length us, event | category | flops | bytes accessed | tf_op | source)
XLA Modules:
  0.0 61.6 jit_solution(14663994586300333795)
XLA Ops:
  0.0 60.9 %layer.1 = bf16[32,8,128]{2,1,0:T(8,128)(2,1)S(1)} custom-call(s32[2]{0:T(128)} %len_hbm.1, bf16[2,2,4096]{2,1,0:T(2,128)(2,1)} %q_hbm.1, bf16[2,2,512]{2,1,0:T(2,128)(2,1)} %nk_hbm.1, bf16[2,2,512]{2,1,0:T(2,128)(2,1)} %nv_hbm.1, bf16[2,384,512]{2,1,0:T(8,128)(2,1)} %k_hbm.1, bf16[2,384,512]{2,1,0:T(8,128)(2,1)} %v_hbm.1, bf16[2,32,512]{2,1,0:T(8,128)(2,1)} %res_hbm.1, ...), custom_call_target="tpu_custom_call" | custom-call | tf_op jit(solution)/shard_map/layer/pallas_call | solution.py:315
  61.0 0.7 %reshape.7 = bf16[2,32,512]{2,1,0:T(8,128)(2,1)} reshape(bf16[2,16,2,4,128]{4,3,2,1,0:T(4,128)(2,1)S(1)} %copy.13) | data formatting | bytes 131072 | tf_op jit(solution)/shard_map/reshape | solution.py:359
  (1 shorter events, 0.0 us)

commit v3 on v2

v3 whole, which is shorter than its diff:
```python
import functools
import math

import jax
import jax.numpy as jnp
from jax import lax
from jax.experimental import pallas as pl
from jax.experimental.pallas import tpu as pltpu
from jax.sharding import PartitionSpec as P

D = 8192
KV = 4
HD = 128
N = 16
SPAN = 384
VERY_LOW = -1e30
F32 = jnp.float32
BF16 = jnp.bfloat16
MESH = pl.DeviceIdType.MESH


def kernel(
    len_hbm, q_hbm, nk_hbm, nv_hbm, k_hbm, v_hbm, res_hbm, ow_hbm, gain_hbm, gw_hbm, uw_hbm, dw_hbm,
    out_ref,
    len_ref, q_v, nk_v, nv_v, k_v, v_v, res_v, ow_v, gain_v, gw_v, uw_v, dw_v,
    qbd, heads, res_s, mid_t,
    st_a, rc_a, st_b, rc_b, st_c, rc_c, st_e32, st_e, rc_e, st_f, rc_f, f32f, st_g, rc_g, st_h,
    load_sem, send_sem, recv_sem, met_sem,
):
    s = lax.axis_index("side")
    r = lax.axis_index("row")
    c = lax.axis_index("col")

    barrier = pltpu.get_barrier_semaphore()

    odd = lax.rem(c, 2)

    def greet_row(i, _):
        pl.semaphore_signal(
            barrier,
            inc=1,
            device_id=(s, lax.rem(r + N // 2 + (i + 1) // 2 * (1 - 2 * lax.rem(i, 2)), N), c - odd + 1),
            device_id_type=MESH,
        )
        return 0

    def greet_col(i, _):
        other = lax.rem(s * N + c + odd + i, 2 * N)
        pl.semaphore_signal(
            barrier, inc=1, device_id=(other // N, r, lax.rem(other, N)), device_id_type=MESH
        )
        return 0

    lax.fori_loop(0, N - 1, greet_row, 0)
    lax.fori_loop(1, N, lambda i, _: greet_col(2 * i, 0), 0)

    @pl.when(odd == 1)
    def _():
        greet_col(0, 0)

    @pl.when(odd == 0)
    def _():
        pl.semaphore_signal(barrier, inc=1, device_id=(s, r, c + 1), device_id_type=MESH)

    loads = [
        pltpu.make_async_copy(src, dst, load_sem.at[i])
        for i, (src, dst) in enumerate(
            [
                (q_hbm, q_v),
                (k_hbm.at[s], k_v),
                (v_hbm.at[s], v_v),
                (nk_hbm, nk_v),
                (nv_hbm, nv_v),
                (res_hbm, res_v),
                (gain_hbm, gain_v),
                (ow_hbm, ow_v),
                (gw_hbm, gw_v),
                (uw_hbm, uw_v),
                (dw_hbm, dw_v),
                (len_hbm, len_ref),
            ]
        )
    ]
    for copy in loads:
        copy.start()

    def met_columns():
        @pl.when(odd == 0)
        def _():
            pl.semaphore_wait(barrier, 2 * N - 1)
            pl.semaphore_signal(met_sem, inc=1, device_id=(s, r, c + 1), device_id_type=MESH)

        @pl.when(odd == 1)
        def _():
            pl.semaphore_wait(met_sem, 1)

    def met_rows():
        @pl.when(odd == 1)
        def _():
            pl.semaphore_wait(barrier, 2 * N - 1)
            pl.semaphore_signal(met_sem, inc=1, device_id=(s, r, c - 1), device_id_type=MESH)

        @pl.when(odd == 0)
        def _():
            pl.semaphore_wait(met_sem, 1)

    def rows_at(ref, at, rows):
        return ref.at[pl.ds(pl.multiple_of(at * rows, rows), rows)]

    def offset(p):
        half = (p + 1) // 2
        return N + half * (2 * lax.rem(p, 2) - 1)

    def place(o):
        return jnp.where(o == 0, 0, jnp.where(o <= N // 2, 2 * o - 1, 2 * (N - o)))

    def send(phase, source, target, device):
        pltpu.make_async_remote_copy(
            src_ref=source,
            dst_ref=target,
            send_sem=send_sem.at[phase],
            recv_sem=recv_sem.at[phase],
            device_id=device,
            device_id_type=MESH,
        ).start()

    def each(first, last, step):
        def one(i, _):
            step(i)
            return 0

        lax.fori_loop(first, last, one, 0)

    def to_columns(phase, source, target):
        def one(i):
            half = (i + 1) // 2
            peer = lax.rem(c + N // 2 + half * (1 - 2 * lax.rem(i, 2)), N)
            send(phase, source(peer), target, (s, r, peer))

        each(0, N - 1, one)

    def arrived(phase, ref):
        pltpu.make_async_copy(ref, ref, recv_sem.at[phase]).wait()

    def sent(phase, ref):
        pltpu.make_async_copy(ref, ref, send_sem.at[phase]).wait()

    qbd[...] = jnp.zeros_like(qbd)
    loads[0].wait()
    query = q_v[...].astype(F32)
    for t in range(2):
        mine = jnp.where(s == 0, query[t, 0:1, :], query[t, 1:2, :])
        for h in range(KV * 8):
            g = h // 8
            one_head = mine[:, h * HD : (h + 1) * HD]
            qbd[2 * h + t : 2 * h + t + 1, g * HD : (g + 1) * HD] = one_head
            heads[h // 2, 2 * (h % 2) + t : 2 * (h % 2) + t + 1, :] = one_head
    loads[1].wait()
    loads[11].wait()
    scale = 1.0 / math.sqrt(HD)
    scores = (
        lax.dot_general(
            qbd[...].astype(BF16), k_v[...], (((1,), (1,)), ((), ())), preferred_element_type=F32
        )
        * scale
    )
    live = c * SPAN + lax.broadcasted_iota(jnp.int32, scores.shape, 1) < len_ref[s]
    scores = jnp.where(live, scores, VERY_LOW)
    peak = jnp.max(scores, axis=1, keepdims=True)
    weights = jnp.where(live, jnp.exp(scores - peak), 0.0)
    total = jnp.sum(weights, axis=1, keepdims=True)
    loads[2].wait()
    summed = jnp.dot(weights.astype(BF16), v_v[...], preferred_element_type=F32)
    low_lane = lax.broadcasted_iota(jnp.int32, (64, HD), 1) < HD // 2
    stats = jnp.where(low_lane, peak, total)
    for o in range(N):
        g = o // 4
        st_a[8 * o : 8 * o + 4, :] = summed[4 * o : 4 * o + 4, g * HD : (g + 1) * HD]
        st_a[8 * o + 4 : 8 * o + 8, :] = stats[4 * o : 4 * o + 4, :]

    met_columns()
    to_columns(0, lambda peer: rows_at(st_a, peer, 8), rows_at(rc_a, c, 8))
    rows_at(rc_a, c, 8)[...] = rows_at(st_a, c, 8)[...]

    group_lanes = pl.ds(pl.multiple_of((c // 4) * HD, HD), HD)
    for copy in loads[3:8]:
        copy.wait()
    q4 = heads[c]
    fresh_k = nk_v[:, :, group_lanes].astype(F32)
    fresh_v = nv_v[:, :, group_lanes].astype(F32)
    nk = [jnp.where(s == 0, fresh_k[t, 0:1, :], fresh_k[t, 1:2, :]) for t in range(2)]
    nv = [jnp.where(s == 0, fresh_v[t, 0:1, :], fresh_v[t, 1:2, :]) for t in range(2)]
    second = lax.rem(lax.broadcasted_iota(jnp.int32, (4, HD), 0), 2) == 1
    f0 = jnp.broadcast_to(jnp.sum(q4 * nk[0], axis=1, keepdims=True) * scale, (4, HD))
    f1 = jnp.broadcast_to(jnp.sum(q4 * nk[1], axis=1, keepdims=True) * scale, (4, HD))
    f1 = jnp.where(second, f1, VERY_LOW)
    at = lax.broadcasted_iota(jnp.int32, (2 * N, 4 * N), 0)
    other = lax.rem(r + offset(at // N * 8 + lax.rem(at, 8)), N)
    wanted = lax.rem(at // 8, 2) * 2 * N + 2 * other + s
    chosen = lax.broadcasted_iota(jnp.int32, (2 * N, 4 * N), 1) == wanted
    res_s[...] = jnp.dot(
        jnp.where(chosen, 1.0, 0.0).astype(BF16), res_v[...].reshape(4 * N, 512), preferred_element_type=F32
    )
    gains = gain_v[...].astype(F32).reshape(1, 512)

    arrived(0, rc_a.at[pl.ds(0, 8 * (N - 1))])
    blocks = rc_a[...].reshape(N, 8, HD)
    sums, stat = blocks[:, 0:4, :], blocks[:, 4:8, :]
    low = lax.broadcasted_iota(jnp.int32, (N, 4, HD), 2) < HD // 2
    turned = pltpu.roll(stat, HD // 2, 2)
    peaks = jnp.where(low, stat, turned)
    totals = jnp.where(low, turned, stat)
    top = jnp.maximum(jnp.max(peaks, axis=0), jnp.maximum(f0, f1))
    share = jnp.exp(peaks - top[None])
    e0 = jnp.exp(f0 - top)
    e1 = jnp.where(second, jnp.exp(f1 - top), 0.0)
    whole = jnp.sum(share * totals, axis=0) + e0 + e1
    mixed = jnp.sum(share * sums, axis=0) + e0 * nv[0] + e1 * nv[1]
    st_b[...] = (mixed / whole).astype(BF16).astype(F32)

    met_rows()
    def give_attended(near):
        def one(i):
            p = (8 if near else N) - 1 - i
            send(1 if near else 2, st_b, rc_b.at[p], (s, lax.rem(r + 2 * N - offset(p), N), c))

        each(0, 7 if near else 8, one)

    give_attended(False)
    give_attended(True)
    rc_b[0] = st_b[...]

    def project(k):
        near = rc_b.at[pl.ds(8 * k, 8)]
        attended = jnp.concatenate(
            [jnp.concatenate([near[:, 2 * j + t, :] for j in range(2)], axis=1) for t in range(2)], axis=0
        )
        st_c[k] = jnp.dot(attended.astype(BF16), ow_v[...], preferred_element_type=F32).astype(BF16)
        to_columns(3 + k, lambda peer: st_c.at[k], rc_c.at[k, c])
        rc_c[k, c] = st_c[k]

    def lift(k):
        mid = res_s[N * k : N * (k + 1), :] + jnp.sum(rc_c[k].astype(F32), axis=0)
        lifted = (mid * gains).astype(BF16)
        squares = jnp.broadcast_to(jnp.sum(mid * mid, axis=1, keepdims=True), (N, HD))
        high = squares.astype(BF16).astype(F32)
        scatter(st_e32, high, 1, 32, 256 * k + 14)
        scatter(st_e32, squares - high, 1, 32, 256 * k + 30)
        if k == 0:
            loads[8].wait()
        scatter(st_e32, jnp.dot(lifted, gw_v[...], preferred_element_type=F32), 7, 32, 256 * k)
        if k == 0:
            loads[9].wait()
        scatter(st_e32, jnp.dot(lifted, uw_v[...], preferred_element_type=F32), 7, 32, 256 * k + 16)
        st_e[256 * k : 256 * (k + 1), :] = st_e32[256 * k : 256 * (k + 1), :].astype(BF16)

        def one(p):
            owner = lax.rem(r + N // 2 + offset(p), N)
            send(5, rows_at(st_e, p, 32), rows_at(rc_e, p, 32), (s, owner, c))

        each(8 * k, 8 + 7 * k, one)
        scatter(mid_t, mid, 4, 8, 64 * k)

    def scatter(ref, value, count, stride, base):
        for t in range(2):
            for m in range(count):
                ref[pl.ds(base + 2 * m + t, 8, stride=stride), :] = value[
                    8 * t : 8 * (t + 1), m * HD : (m + 1) * HD
                ]

    arrived(1, rc_b.at[pl.ds(0, 7)])
    project(0)
    arrived(2, rc_b.at[pl.ds(0, 8)])
    project(1)
    arrived(3, rc_c.at[0, pl.ds(0, N - 1)])
    lift(0)
    arrived(4, rc_c.at[1, pl.ds(0, N - 1)])
    lift(1)
    rc_e[32 * (N - 1) :, :] = st_e[32 * (N - 1) :, :]
    arrived(5, rc_e.at[pl.ds(0, 32 * (N - 1))])
    lifts = jnp.sum(rc_e[...].astype(F32).reshape(N, 32, HD), axis=0)
    gate, up = lifts[0:16], lifts[16:32]
    inv0 = lax.rsqrt((gate[14:15] + up[14:15]) / D + 1e-05)
    inv1 = lax.rsqrt((gate[15:16] + up[15:16]) / D + 1e-05)
    inv = jnp.where(lax.rem(lax.broadcasted_iota(jnp.int32, (16, HD), 0), 2) == 1, inv1, inv0)
    gate, up = gate * inv, up * inv
    st_f[...] = (gate / (1.0 + jnp.exp(-gate)) * up).astype(BF16)

    def give_act(i):
        p = N - 1 - i
        send(6, st_f, rows_at(rc_f, p, 16), (s, lax.rem(r + 2 * N - offset(p), N), c))

    each(0, N - 1, give_act)
    rc_f[0:16, :] = st_f[...]
    loads[10].wait()
    arrived(6, rc_f.at[pl.ds(0, 16 * (N - 1))])
    f32f[...] = rc_f[...].astype(F32)
    act = jnp.concatenate(
        [
            jnp.concatenate([f32f[pl.ds(2 * m + t, N, stride=16), :] for m in range(7)], axis=1)
            for t in range(2)
        ],
        axis=0,
    )
    part = jnp.dot(act.astype(BF16), dw_v[...], preferred_element_type=F32)
    for t in range(2):
        for m in range(4):
            st_g[pl.ds(2 * m + t, N, stride=8), :] = part[N * t : N * (t + 1), m * HD : (m + 1) * HD]

    def act_place(row):
        return place(lax.rem(row + N + N // 2 - r, N))

    to_columns(7, lambda peer: rows_at(st_g, act_place(peer), 8), rows_at(rc_g, c, 8))
    rows_at(rc_g, c, 8)[...] = rows_at(st_g, act_place(c), 8)[...]
    arrived(7, rc_g.at[pl.ds(0, 8 * (N - 1))])
    mid_piece = rows_at(mid_t, place(lax.rem(c + N - r, N)), 8)[...]
    st_h[...] = (mid_piece + jnp.sum(rc_g[...].reshape(N, 8, HD), axis=0)).astype(BF16)
    here = s * N + c

    def give(i):
        other = lax.rem(here + i, 2 * N)
        send(8, st_h, out_ref.at[here], (other // N, r, lax.rem(other, N)))

    each(1, 2 * N, give)
    out_ref[here] = st_h[...]

    sent(0, rc_a.at[pl.ds(0, 8 * (N - 1))])
    sent(1, rc_b.at[pl.ds(0, 7)])
    sent(2, rc_b.at[pl.ds(0, 8)])
    sent(3, rc_c.at[0, pl.ds(0, N - 1)])
    sent(4, rc_c.at[1, pl.ds(0, N - 1)])
    sent(5, rc_e.at[pl.ds(0, 32 * (N - 1))])
    sent(6, rc_f.at[pl.ds(0, 16 * (N - 1))])
    sent(7, rc_g.at[pl.ds(0, 8 * (N - 1))])
    arrived(8, out_ref.at[pl.ds(0, 2 * N - 1)])
    sent(8, out_ref.at[pl.ds(0, 2 * N - 1)])


def shards(query, new_keys, new_values, key_cache, value_cache, lengths, residual, out_weight,
           norm_gain, gate_weight, up_weight, down_weight):
    def vm(*shape, kind=F32):
        return pltpu.VMEM(shape, kind)

    hbm = pl.BlockSpec(memory_space=pltpu.HBM)
    pieces = pl.pallas_call(
        kernel,
        out_shape=jax.ShapeDtypeStruct((2 * N, 8, HD), BF16),
        in_specs=[hbm] * 12,
        out_specs=pl.BlockSpec(memory_space=pltpu.VMEM),
        scratch_shapes=[
            pltpu.SMEM((2,), jnp.int32),
            vm(2, 2, 4096, kind=BF16),
            vm(2, 2, 512, kind=BF16),
            vm(2, 2, 512, kind=BF16),
            vm(SPAN, 512, kind=BF16),
            vm(SPAN, 512, kind=BF16),
            vm(2, 32, 512, kind=BF16),
            vm(256, 512, kind=BF16),
            vm(512, kind=BF16),
            vm(512, 896, kind=BF16),
            vm(512, 896, kind=BF16),
            vm(896, 512, kind=BF16),
            vm(64, 512),
            vm(N, 4, HD),
            vm(2 * N, 512),
            vm(8 * N, HD),
            vm(8 * N, HD), vm(8 * N, HD),
            vm(4, HD), vm(N, 4, HD),
            vm(2, N, 512, kind=BF16), vm(2, N, N, 512, kind=BF16),
            vm(32 * N, HD), vm(32 * N, HD, kind=BF16), vm(32 * N, HD, kind=BF16),
            vm(16, HD, kind=BF16), vm(16 * N, HD, kind=BF16), vm(16 * N, HD),
            vm(8 * N, HD), vm(8 * N, HD),
            vm(8, HD, kind=BF16),
            pltpu.SemaphoreType.DMA((12,)),
            pltpu.SemaphoreType.DMA((9,)),
            pltpu.SemaphoreType.DMA((9,)),
            pltpu.SemaphoreType.REGULAR,
        ],
        compiler_params=pltpu.CompilerParams(
            collective_id=0, has_side_effects=True, vmem_limit_bytes=32 * 1024 * 1024
        ),
        name="layer",
    )(*[
        pltpu.with_memory_space_constraint(a, pltpu.HBM)
        for a in (lengths, query, new_keys, new_values, key_cache, value_cache, residual, out_weight,
                  norm_gain, gate_weight, up_weight, down_weight)
    ])
    pieces = pieces.reshape(2, N, 4, 2, HD)
    return pieces.transpose(3, 1, 0, 2, 4).reshape(2, 2 * N, 512)


def solution(mesh):
    in_specs = (
        P(None, "row", None),
        P(None, "row", None),
        P(None, "row", None),
        P("row", "col", None),
        P("row", "col", None),
        P("row"),
        P(None, None, "row"),
        P("col", "row"),
        P("row"),
        P("row", "col"),
        P("row", "col"),
        P("col", "row"),
    )
    out_specs = P(None, None, "row")
    return jax.shard_map(shards, mesh=mesh, in_specs=in_specs, out_specs=out_specs, check_vma=False)
```

time: 61.7 us -> 58 us (0.940)
  Pallas kernels: 60.9 us -> 57.2 us
    pallas_call x1, Pallas kernels: 60.9 us -> 57.2 us  [shards(): pl.pallas_call(kernel, out_shape=jax.ShapeDtypeStruct((2 * N, 8, HD), BF1...]
where the time goes in v3:
time: 58 us; the launch traced here: 57.9 us
  Pallas kernels  57.2 us (99%)
  local copies, waits for them, and re-layouts  0.68 us (1%)
    pallas_call x1, Pallas kernels, shards(): pl.pallas_call(kernel, out_shape=jax.ShapeDtypeStruct((2 * N, 8, HD), BF1...  57.2 us

profile of v3, /device:TPU:1, one launch (start us, length us, event | category | flops | bytes accessed | tf_op | source)
XLA Modules:
  0.0 57.9 jit_solution(3588087039383505555)
XLA Ops:
  0.0 57.2 %layer.1 = bf16[32,8,128]{2,1,0:T(8,128)(2,1)S(1)} custom-call(s32[2]{0:T(128)} %len_hbm.1, bf16[2,2,4096]{2,1,0:T(2,128)(2,1)} %q_hbm.1, bf16[2,2,512]{2,1,0:T(2,128)(2,1)} %nk_hbm.1, bf16[2,2,512]{2,1,0:T(2,128)(2,1)} %nv_hbm.1, bf16[2,384,512]{2,1,0:T(8,128)(2,1)} %k_hbm.1, bf16[2,384,512]{2,1,0:T(8,128)(2,1)} %v_hbm.1, bf16[2,32,512]{2,1,0:T(8,128)(2,1)} %res_hbm.1, ...), custom_call_target="tpu_custom_call" | custom-call | tf_op jit(solution)/shard_map/layer/pallas_call | solution.py:345
  57.2 0.7 %reshape.7 = bf16[2,32,512]{2,1,0:T(8,128)(2,1)} reshape(bf16[2,16,2,4,128]{4,3,2,1,0:T(4,128)(2,1)S(1)} %copy.13) | data formatting | bytes 131072 | tf_op jit(solution)/shard_map/reshape | solution.py:389
  (1 shorter events, 0.0 us)

commit v4 on v3

--- a/solution.py
+++ b/solution.py
@@ -45,22 +45,28 @@
         return 0
 
     def greet_col(i, _):
-        other = lax.rem(s * N + c + odd + i, 2 * N)
         pl.semaphore_signal(
-            barrier, inc=1, device_id=(other // N, r, lax.rem(other, N)), device_id_type=MESH
+            barrier, inc=1, device_id=(s, r, lax.rem(c + odd + 2 * i, N)), device_id_type=MESH
         )
         return 0
 
+    def greet_side(i, _):
+        pl.semaphore_signal(barrier, inc=1, device_id=(1 - s, r, 2 * i + 1), device_id_type=MESH)
+        return 0
+
     lax.fori_loop(0, N - 1, greet_row, 0)
-    lax.fori_loop(1, N, lambda i, _: greet_col(2 * i, 0), 0)
 
     @pl.when(odd == 1)
     def _():
         greet_col(0, 0)
 
+    lax.fori_loop(1, N // 2, greet_col, 0)
+
     @pl.when(odd == 0)
     def _():
         pl.semaphore_signal(barrier, inc=1, device_id=(s, r, c + 1), device_id_type=MESH)
+
+    lax.fori_loop(0, N // 2, greet_side, 0)
 
     loads = [
         pltpu.make_async_copy(src, dst, load_sem.at[i])
@@ -87,7 +93,7 @@
     def met_columns():
         @pl.when(odd == 0)
         def _():
-            pl.semaphore_wait(barrier, 2 * N - 1)
+            pl.semaphore_wait(barrier, N - 1)
             pl.semaphore_signal(met_sem, inc=1, device_id=(s, r, c + 1), device_id_type=MESH)
 
         @pl.when(odd == 1)
@@ -97,7 +103,7 @@
     def met_rows():
         @pl.when(odd == 1)
         def _():
-            pl.semaphore_wait(barrier, 2 * N - 1)
+            pl.semaphore_wait(barrier, 3 * N - 1)
             pl.semaphore_signal(met_sem, inc=1, device_id=(s, r, c - 1), device_id_type=MESH)
 
         @pl.when(odd == 0)
@@ -195,8 +201,8 @@
     f1 = jnp.broadcast_to(jnp.sum(q4 * nk[1], axis=1, keepdims=True) * scale, (4, HD))
     f1 = jnp.where(second, f1, VERY_LOW)
     at = lax.broadcasted_iota(jnp.int32, (2 * N, 4 * N), 0)
-    other = lax.rem(r + offset(at // N * 8 + lax.rem(at, 8)), N)
-    wanted = lax.rem(at // 8, 2) * 2 * N + 2 * other + s
+    other = lax.rem(r + offset(at // 8 * 4 + lax.rem(at, 4)), N)
+    wanted = lax.rem(at // 4, 2) * 2 * N + 2 * other + s
     chosen = lax.broadcasted_iota(jnp.int32, (2 * N, 4 * N), 1) == wanted
     res_s[...] = jnp.dot(
         jnp.where(chosen, 1.0, 0.0).astype(BF16), res_v[...].reshape(4 * N, 512), preferred_element_type=F32
@@ -219,65 +225,77 @@
     st_b[...] = (mixed / whole).astype(BF16).astype(F32)
 
     met_rows()
-    def give_attended(near):
+    def give_attended(k):
         def one(i):
-            p = (8 if near else N) - 1 - i
-            send(1 if near else 2, st_b, rc_b.at[p], (s, lax.rem(r + 2 * N - offset(p), N), c))
-
-        each(0, 7 if near else 8, one)
-
-    give_attended(False)
-    give_attended(True)
+            p = 4 * k + 3 - i
+            send(1 + k, st_b, rc_b.at[p], (s, lax.rem(r + 2 * N - offset(p), N), c))
+
+        each(0, 4 if k else 3, one)
+
+    for k in range(3, -1, -1):
+        give_attended(k)
     rc_b[0] = st_b[...]
 
     def project(k):
-        near = rc_b.at[pl.ds(8 * k, 8)]
         attended = jnp.concatenate(
-            [jnp.concatenate([near[:, 2 * j + t, :] for j in range(2)], axis=1) for t in range(2)], axis=0
+            [
+                jnp.concatenate([rc_b[4 * k : 4 * k + 4, 2 * j + t, :] for j in range(2)], axis=1)
+                for t in range(2)
+            ],
+            axis=0,
         )
         st_c[k] = jnp.dot(attended.astype(BF16), ow_v[...], preferred_element_type=F32).astype(BF16)
-        to_columns(3 + k, lambda peer: st_c.at[k], rc_c.at[k, c])
+        to_columns(5 + k, lambda peer: st_c.at[k], rc_c.at[k, c])
         rc_c[k, c] = st_c[k]
-
-    def lift(k):
-        mid = res_s[N * k : N * (k + 1), :] + jnp.sum(rc_c[k].astype(F32), axis=0)
-        lifted = (mid * gains).astype(BF16)
-        squares = jnp.broadcast_to(jnp.sum(mid * mid, axis=1, keepdims=True), (N, HD))
-        high = squares.astype(BF16).astype(F32)
-        scatter(st_e32, high, 1, 32, 256 * k + 14)
-        scatter(st_e32, squares - high, 1, 32, 256 * k + 30)
-        if k == 0:
-            loads[8].wait()
-        scatter(st_e32, jnp.dot(lifted, gw_v[...], preferred_element_type=F32), 7, 32, 256 * k)
-        if k == 0:
-            loads[9].wait()
-        scatter(st_e32, jnp.dot(lifted, uw_v[...], preferred_element_type=F32), 7, 32, 256 * k + 16)
-        st_e[256 * k : 256 * (k + 1), :] = st_e32[256 * k : 256 * (k + 1), :].astype(BF16)
-
-        def one(p):
-            owner = lax.rem(r + N // 2 + offset(p), N)
-            send(5, rows_at(st_e, p, 32), rows_at(rc_e, p, 32), (s, owner, c))
-
-        each(8 * k, 8 + 7 * k, one)
-        scatter(mid_t, mid, 4, 8, 64 * k)
 
     def scatter(ref, value, count, stride, base):
         for t in range(2):
             for m in range(count):
-                ref[pl.ds(base + 2 * m + t, 8, stride=stride), :] = value[
-                    8 * t : 8 * (t + 1), m * HD : (m + 1) * HD
+                ref[pl.ds(base + 2 * m + t, 4, stride=stride), :] = value[
+                    4 * t : 4 * (t + 1), m * HD : (m + 1) * HD
                 ]
 
-    arrived(1, rc_b.at[pl.ds(0, 7)])
+    def lift(k):
+        mid = res_s[8 * k : 8 * (k + 1), :] + jnp.sum(rc_c[k].astype(F32), axis=0)
+        lifted = (mid * gains).astype(BF16)
+        squares = jnp.broadcast_to(jnp.sum(mid * mid, axis=1, keepdims=True), (8, HD))
+        high = squares.astype(BF16).astype(F32)
+        base = 128 * k
+        scatter(st_e32, high, 1, 32, base + 14)
+        scatter(st_e32, squares - high, 1, 32, base + 30)
+        if k == 0:
+            loads[8].wait()
+        scatter(st_e32, jnp.dot(lifted, gw_v[...], preferred_element_type=F32), 7, 32, base)
+        if k == 0:
+            loads[9].wait()
+        scatter(st_e32, jnp.dot(lifted, uw_v[...], preferred_element_type=F32), 7, 32, base + 16)
+        st_e[base : base + 128, :] = st_e32[base : base + 128, :].astype(BF16)
+
+        def one(p):
+            owner = lax.rem(r + N // 2 + offset(p), N)
+            send(9, rows_at(st_e, p, 32), rows_at(rc_e, p, 32), (s, owner, c))
+
+        each(4 * k, 4 * k + (4 if k < 3 else 3), one)
+        scatter(mid_t, mid, 4, 8, 32 * k)
+
+    arrived(1, rc_b.at[pl.ds(0, 3)])
     project(0)
-    arrived(2, rc_b.at[pl.ds(0, 8)])
+    arrived(2, rc_b.at[pl.ds(0, 4)])
     project(1)
-    arrived(3, rc_c.at[0, pl.ds(0, N - 1)])
+    arrived(3, rc_b.at[pl.ds(0, 4)])
+    project(2)
+    arrived(4, rc_b.at[pl.ds(0, 4)])
+    project(3)
+    arrived(5, rc_c.at[0, pl.ds(0, N - 1)])
     lift(0)
-    arrived(4, rc_c.at[1, pl.ds(0, N - 1)])
+    arrived(6, rc_c.at[1, pl.ds(0, N - 1)])
     lift(1)
+    arrived(7, rc_c.at[2, pl.ds(0, N - 1)])
+    lift(2)
+    arrived(8, rc_c.at[3, pl.ds(0, N - 1)])
+    lift(3)
     rc_e[32 * (N - 1) :, :] = st_e[32 * (N - 1) :, :]
-    arrived(5, rc_e.at[pl.ds(0, 32 * (N - 1))])
+    arrived(9, rc_e.at[pl.ds(0, 32 * (N - 1))])
     lifts = jnp.sum(rc_e[...].astype(F32).reshape(N, 32, HD), axis=0)
     gate, up = lifts[0:16], lifts[16:32]
     inv0 = lax.rsqrt((gate[14:15] + up[14:15]) / D + 1e-05)
@@ -288,12 +306,12 @@
 
     def give_act(i):
         p = N - 1 - i
-        send(6, st_f, rows_at(rc_f, p, 16), (s, lax.rem(r + 2 * N - offset(p), N), c))
+        send(10, st_f, rows_at(rc_f, p, 16), (s, lax.rem(r + 2 * N - offset(p), N), c))
 
     each(0, N - 1, give_act)
     rc_f[0:16, :] = st_f[...]
     loads[10].wait()
-    arrived(6, rc_f.at[pl.ds(0, 16 * (N - 1))])
+    arrived(10, rc_f.at[pl.ds(0, 16 * (N - 1))])
     f32f[...] = rc_f[...].astype(F32)
     act = jnp.concatenate(
         [
@@ -310,30 +328,34 @@
     def act_place(row):
         return place(lax.rem(row + N + N // 2 - r, N))
 
-    to_columns(7, lambda peer: rows_at(st_g, act_place(peer), 8), rows_at(rc_g, c, 8))
+    to_columns(11, lambda peer: rows_at(st_g, act_place(peer), 8), rows_at(rc_g, c, 8))
     rows_at(rc_g, c, 8)[...] = rows_at(st_g, act_place(c), 8)[...]
-    arrived(7, rc_g.at[pl.ds(0, 8 * (N - 1))])
+    arrived(11, rc_g.at[pl.ds(0, 8 * (N - 1))])
     mid_piece = rows_at(mid_t, place(lax.rem(c + N - r, N)), 8)[...]
     st_h[...] = (mid_piece + jnp.sum(rc_g[...].reshape(N, 8, HD), axis=0)).astype(BF16)
     here = s * N + c
 
     def give(i):
         other = lax.rem(here + i, 2 * N)
-        send(8, st_h, out_ref.at[here], (other // N, r, lax.rem(other, N)))
+        send(12, st_h, out_ref.at[here], (other // N, r, lax.rem(other, N)))
 
     each(1, 2 * N, give)
     out_ref[here] = st_h[...]
 
     sent(0, rc_a.at[pl.ds(0, 8 * (N - 1))])
-    sent(1, rc_b.at[pl.ds(0, 7)])
-    sent(2, rc_b.at[pl.ds(0, 8)])
-    sent(3, rc_c.at[0, pl.ds(0, N - 1)])
-    sent(4, rc_c.at[1, pl.ds(0, N - 1)])
-    sent(5, rc_e.at[pl.ds(0, 32 * (N - 1))])
-    sent(6, rc_f.at[pl.ds(0, 16 * (N - 1))])
-    sent(7, rc_g.at[pl.ds(0, 8 * (N - 1))])
-    arrived(8, out_ref.at[pl.ds(0, 2 * N - 1)])
-    sent(8, out_ref.at[pl.ds(0, 2 * N - 1)])
+    sent(1, rc_b.at[pl.ds(0, 3)])
+    sent(2, rc_b.at[pl.ds(0, 4)])
+    sent(3, rc_b.at[pl.ds(0, 4)])
+    sent(4, rc_b.at[pl.ds(0, 4)])
+    sent(5, rc_c.at[0, pl.ds(0, N - 1)])
+    sent(6, rc_c.at[1, pl.ds(0, N - 1)])
+    sent(7, rc_c.at[2, pl.ds(0, N - 1)])
+    sent(8, rc_c.at[3, pl.ds(0, N - 1)])
+    sent(9, rc_e.at[pl.ds(0, 32 * (N - 1))])
+    sent(10, rc_f.at[pl.ds(0, 16 * (N - 1))])
+    sent(11, rc_g.at[pl.ds(0, 8 * (N - 1))])
+    arrived(12, out_ref.at[pl.ds(0, 2 * N - 1)])
+    sent(12, out_ref.at[pl.ds(0, 2 * N - 1)])
 
 
 def shards(query, new_keys, new_values, key_cache, value_cache, lengths, residual, out_weight,
@@ -366,14 +388,14 @@
             vm(8 * N, HD),
             vm(8 * N, HD), vm(8 * N, HD),
             vm(4, HD), vm(N, 4, HD),
-            vm(2, N, 512, kind=BF16), vm(2, N, N, 512, kind=BF16),
+            vm(4, 8, 512, kind=BF16), vm(4, N, 8, 512, kind=BF16),
             vm(32 * N, HD), vm(32 * N, HD, kind=BF16), vm(32 * N, HD, kind=BF16),
             vm(16, HD, kind=BF16), vm(16 * N, HD, kind=BF16), vm(16 * N, HD),
             vm(8 * N, HD), vm(8 * N, HD),
             vm(8, HD, kind=BF16),
             pltpu.SemaphoreType.DMA((12,)),
-            pltpu.SemaphoreType.DMA((9,)),
-            pltpu.SemaphoreType.DMA((9,)),
+            pltpu.SemaphoreType.DMA((13,)),
+            pltpu.SemaphoreType.DMA((13,)),
             pltpu.SemaphoreType.REGULAR,
         ],
         compiler_params=pltpu.CompilerParams(

time: 58 us -> 55 us (0.948)
  Pallas kernels: 57.2 us -> 54.2 us
    pallas_call x1, Pallas kernels: 57.2 us -> 54.2 us  [shards(): pl.pallas_call(kernel, out_shape=jax.ShapeDtypeStruct((2 * N, 8, HD), BF1...]
where the time goes in v4:
time: 55 us; the launch traced here: 54.9 us
  Pallas kernels  54.2 us (99%)
  local copies, waits for them, and re-layouts  0.68 us (1%)
    pallas_call x1, Pallas kernels, shards(): pl.pallas_call(kernel, out_shape=jax.ShapeDtypeStruct((2 * N, 8, HD), BF1...  54.2 us

profile of v4, /device:TPU:1, one launch (start us, length us, event | category | flops | bytes accessed | tf_op | source)
XLA Modules:
  0.0 54.9 jit_solution(7736800350537387978)
XLA Ops:
  0.0 54.2 %layer.1 = bf16[32,8,128]{2,1,0:T(8,128)(2,1)S(1)} custom-call(s32[2]{0:T(128)} %len_hbm.1, bf16[2,2,4096]{2,1,0:T(2,128)(2,1)} %q_hbm.1, bf16[2,2,512]{2,1,0:T(2,128)(2,1)} %nk_hbm.1, bf16[2,2,512]{2,1,0:T(2,128)(2,1)} %nv_hbm.1, bf16[2,384,512]{2,1,0:T(8,128)(2,1)} %k_hbm.1, bf16[2,384,512]{2,1,0:T(8,128)(2,1)} %v_hbm.1, bf16[2,32,512]{2,1,0:T(8,128)(2,1)} %res_hbm.1, ...), custom_call_target="tpu_custom_call" | custom-call | tf_op jit(solution)/shard_map/layer/pallas_call | solution.py:367
  54.2 0.7 %reshape.7 = bf16[2,32,512]{2,1,0:T(8,128)(2,1)} reshape(bf16[2,16,2,4,128]{4,3,2,1,0:T(4,128)(2,1)S(1)} %copy.13) | data formatting | bytes 131072 | tf_op jit(solution)/shard_map/reshape | solution.py:411
  (1 shorter events, 0.0 us)

commit v5 on v4

--- a/solution.py
+++ b/solution.py
@@ -24,7 +24,7 @@
     out_ref,
     len_ref, q_v, nk_v, nv_v, k_v, v_v, res_v, ow_v, gain_v, gw_v, uw_v, dw_v,
     qbd, heads, res_s, mid_t,
-    st_a, rc_a, st_b, rc_b, st_c, rc_c, st_e32, st_e, rc_e, st_f, rc_f, f32f, st_g, rc_g, st_h,
+    st_a, rc_a, st_b, rc_b, st_c, rc_c, st_e32, st_e, rc_e, st_f, rc_f, f32f, st_p, rc_p, kept, st_g, rc_g, both, order,
     load_sem, send_sem, recv_sem, met_sem,
 ):
     s = lax.axis_index("side")
@@ -34,6 +34,7 @@
     barrier = pltpu.get_barrier_semaphore()
 
     odd = lax.rem(c, 2)
+    partner = c + 1 - 2 * odd
 
     def greet_row(i, _):
         pl.semaphore_signal(
@@ -116,9 +117,6 @@
     def offset(p):
         half = (p + 1) // 2
         return N + half * (2 * lax.rem(p, 2) - 1)
-
-    def place(o):
-        return jnp.where(o == 0, 0, jnp.where(o <= N // 2, 2 * o - 1, 2 * (N - o)))
 
     def send(phase, source, target, device):
         pltpu.make_async_remote_copy(
@@ -276,7 +274,15 @@
             send(9, rows_at(st_e, p, 32), rows_at(rc_e, p, 32), (s, owner, c))
 
         each(4 * k, 4 * k + (4 if k < 3 else 3), one)
-        scatter(mid_t, mid, 4, 8, 32 * k)
+        half = own_half(mid)
+        at = 4 * s + 3 - k
+        for t in range(2):
+            for i in range(4):
+                mid_t[at, 4 * t + 3 - i : 4 * t + 4 - i, :] = half[4 * t + i : 4 * t + i + 1, :]
+        send(22, mid_t.at[at], mid_t.at[at], (1 - s, r, c))
+
+    def own_half(value):
+        return jnp.where(odd == 0, value[:, :256], value[:, 256:])
 
     arrived(1, rc_b.at[pl.ds(0, 3)])
     project(0)
@@ -304,43 +310,87 @@
     gate, up = gate * inv, up * inv
     st_f[...] = (gate / (1.0 + jnp.exp(-gate)) * up).astype(BF16)
 
-    def give_act(i):
-        p = N - 1 - i
-        send(10, st_f, rows_at(rc_f, p, 16), (s, lax.rem(r + 2 * N - offset(p), N), c))
-
-    each(0, N - 1, give_act)
+    def give_act(k):
+        def one(i):
+            p = 4 * k + 3 - i
+            send(10 + k, st_f, rows_at(rc_f, p, 16), (s, lax.rem(r + 2 * N - offset(p), N), c))
+
+        each(0, 4 if k else 3, one)
+
+    for k in range(3, -1, -1):
+        give_act(k)
     rc_f[0:16, :] = st_f[...]
+    target = lax.broadcasted_iota(jnp.int32, (4 * N, 4 * N), 0)
+    source = lax.broadcasted_iota(jnp.int32, (4 * N, 4 * N), 1)
+    row = lax.rem(r + N // 2 + offset(source // 16 * 4 + lax.rem(source, 4)), N)
+    lands = lax.rem(source // 4, 2) * 2 * N + 2 * row + lax.rem(source // 8, 2)
+    order[...] = jnp.where(target == lands, 1.0, 0.0).astype(BF16)
     loads[10].wait()
-    arrived(10, rc_f.at[pl.ds(0, 16 * (N - 1))])
-    f32f[...] = rc_f[...].astype(F32)
-    act = jnp.concatenate(
-        [
-            jnp.concatenate([f32f[pl.ds(2 * m + t, N, stride=16), :] for m in range(7)], axis=1)
-            for t in range(2)
-        ],
-        axis=0,
-    )
-    part = jnp.dot(act.astype(BF16), dw_v[...], preferred_element_type=F32)
-    for t in range(2):
-        for m in range(4):
-            st_g[pl.ds(2 * m + t, N, stride=8), :] = part[N * t : N * (t + 1), m * HD : (m + 1) * HD]
-
-    def act_place(row):
-        return place(lax.rem(row + N + N // 2 - r, N))
-
-    to_columns(11, lambda peer: rows_at(st_g, act_place(peer), 8), rows_at(rc_g, c, 8))
-    rows_at(rc_g, c, 8)[...] = rows_at(st_g, act_place(c), 8)[...]
-    arrived(11, rc_g.at[pl.ds(0, 8 * (N - 1))])
-    mid_piece = rows_at(mid_t, place(lax.rem(c + N - r, N)), 8)[...]
-    st_h[...] = (mid_piece + jnp.sum(rc_g[...].reshape(N, 8, HD), axis=0)).astype(BF16)
-    here = s * N + c
-
-    def give(i):
-        other = lax.rem(here + i, 2 * N)
-        send(12, st_h, out_ref.at[here], (other // N, r, lax.rem(other, N)))
-
-    each(1, 2 * N, give)
-    out_ref[here] = st_h[...]
+
+    def down(k):
+        f32f[64 * k : 64 * (k + 1), :] = rc_f[64 * k : 64 * (k + 1), :].astype(F32)
+        act = jnp.concatenate(
+            [
+                jnp.concatenate(
+                    [f32f[pl.ds(64 * k + 2 * m + t, 4, stride=16), :] for m in range(7)], axis=1
+                )
+                for t in range(2)
+            ],
+            axis=0,
+        )
+        part = jnp.dot(act.astype(BF16), dw_v[...], preferred_element_type=F32)
+        st_p[k] = jnp.where(odd == 0, part[:, 256:], part[:, :256])
+        send(14 + k, st_p.at[k], rc_p.at[k], (s, r, partner))
+        kept[k] = own_half(part)
+
+    spot = s * (N // 2) + c // 2
+
+    def merge(k):
+        st_g[k] = (kept[k] + rc_p[k]).astype(BF16)
+
+        def one(i):
+            other = lax.rem(spot + i, N)
+            peer = (other // (N // 2), r, 2 * lax.rem(other, N // 2) + odd)
+            send(18 + k, st_g.at[k], rc_g.at[k, spot], peer)
+
+        each(1, N, one)
+        rc_g[k, spot] = st_g[k]
+
+    def finish(k):
+        for side in range(2):
+            parts = jnp.sum(rc_g[k, 8 * side : 8 * side + 8].astype(F32), axis=0)
+            both[odd, k, side] = (mid_t[4 * side + k] + parts).astype(BF16)
+        send(23, both.at[odd, k], both.at[odd, k], (s, r, partner))
+
+    arrived(10, rc_f.at[pl.ds(0, 48)])
+    down(0)
+    arrived(11, rc_f.at[pl.ds(0, 64)])
+    down(1)
+    arrived(14, rc_p.at[0])
+    merge(0)
+    arrived(12, rc_f.at[pl.ds(0, 64)])
+    down(2)
+    arrived(15, rc_p.at[1])
+    merge(1)
+    arrived(13, rc_f.at[pl.ds(0, 64)])
+    down(3)
+    arrived(16, rc_p.at[2])
+    merge(2)
+    arrived(17, rc_p.at[3])
+    merge(3)
+    arrived(22, mid_t.at[pl.ds(0, 4)])
+    arrived(18, rc_g.at[0, pl.ds(0, N - 1)])
+    finish(0)
+    arrived(19, rc_g.at[1, pl.ds(0, N - 1)])
+    finish(1)
+    arrived(20, rc_g.at[2, pl.ds(0, N - 1)])
+    finish(2)
+    arrived(21, rc_g.at[3, pl.ds(0, N - 1)])
+    finish(3)
+    arrived(23, both.at[0])
+    rows = jnp.concatenate([both[h].astype(F32).reshape(4 * N, 256) for h in range(2)], axis=1)
+    result = jnp.dot(order[...], rows.astype(BF16), preferred_element_type=F32)
+    out_ref[...] = result.astype(BF16).reshape(2, 2 * N, 512)
 
     sent(0, rc_a.at[pl.ds(0, 8 * (N - 1))])
     sent(1, rc_b.at[pl.ds(0, 3)])
@@ -352,10 +402,20 @@
     sent(7, rc_c.at[2, pl.ds(0, N - 1)])
     sent(8, rc_c.at[3, pl.ds(0, N - 1)])
     sent(9, rc_e.at[pl.ds(0, 32 * (N - 1))])
-    sent(10, rc_f.at[pl.ds(0, 16 * (N - 1))])
-    sent(11, rc_g.at[pl.ds(0, 8 * (N - 1))])
-    arrived(12, out_ref.at[pl.ds(0, 2 * N - 1)])
-    sent(12, out_ref.at[pl.ds(0, 2 * N - 1)])
+    sent(10, rc_f.at[pl.ds(0, 48)])
+    sent(11, rc_f.at[pl.ds(0, 64)])
+    sent(12, rc_f.at[pl.ds(0, 64)])
+    sent(13, rc_f.at[pl.ds(0, 64)])
+    sent(14, rc_p.at[0])
+    sent(15, rc_p.at[1])
+    sent(16, rc_p.at[2])
+    sent(17, rc_p.at[3])
+    sent(18, rc_g.at[0, pl.ds(0, N - 1)])
+    sent(19, rc_g.at[1, pl.ds(0, N - 1)])
+    sent(20, rc_g.at[2, pl.ds(0, N - 1)])
+    sent(21, rc_g.at[3, pl.ds(0, N - 1)])
+    sent(22, mid_t.at[pl.ds(0, 4)])
+    sent(23, both.at[0])
 
 
 def shards(query, new_keys, new_values, key_cache, value_cache, lengths, residual, out_weight,
@@ -364,9 +424,9 @@
         return pltpu.VMEM(shape, kind)
 
     hbm = pl.BlockSpec(memory_space=pltpu.HBM)
-    pieces = pl.pallas_call(
+    return pl.pallas_call(
         kernel,
-        out_shape=jax.ShapeDtypeStruct((2 * N, 8, HD), BF16),
+        out_shape=jax.ShapeDtypeStruct((2, 2 * N, 512), BF16),
         in_specs=[hbm] * 12,
         out_specs=pl.BlockSpec(memory_space=pltpu.VMEM),
         scratch_shapes=[
@@ -385,17 +445,19 @@
             vm(64, 512),
             vm(N, 4, HD),
             vm(2 * N, 512),
-            vm(8 * N, HD),
+            vm(8, 8, 256),
             vm(8 * N, HD), vm(8 * N, HD),
             vm(4, HD), vm(N, 4, HD),
             vm(4, 8, 512, kind=BF16), vm(4, N, 8, 512, kind=BF16),
             vm(32 * N, HD), vm(32 * N, HD, kind=BF16), vm(32 * N, HD, kind=BF16),
             vm(16, HD, kind=BF16), vm(16 * N, HD, kind=BF16), vm(16 * N, HD),
-            vm(8 * N, HD), vm(8 * N, HD),
-            vm(8, HD, kind=BF16),
+            vm(4, 8, 256), vm(4, 8, 256), vm(4, 8, 256),
+            vm(4, 8, 256, kind=BF16), vm(4, N, 8, 256, kind=BF16),
+            vm(2, 4, 2, 8, 256, kind=BF16),
+            vm(4 * N, 4 * N, kind=BF16),
             pltpu.SemaphoreType.DMA((12,)),
-            pltpu.SemaphoreType.DMA((13,)),
-            pltpu.SemaphoreType.DMA((13,)),
+            pltpu.SemaphoreType.DMA((24,)),
+            pltpu.SemaphoreType.DMA((24,)),
             pltpu.SemaphoreType.REGULAR,
         ],
         compiler_params=pltpu.CompilerParams(
@@ -407,8 +469,6 @@
         for a in (lengths, query, new_keys, new_values, key_cache, value_cache, residual, out_weight,
                   norm_gain, gate_weight, up_weight, down_weight)
     ])
-    pieces = pieces.reshape(2, N, 4, 2, HD)
-    return pieces.transpose(3, 1, 0, 2, 4).reshape(2, 2 * N, 512)
 
 
 def solution(mesh):

time: 55 us -> 53.1 us (0.965)
  Pallas kernels: 54.2 us -> 52.3 us
    pallas_call x1, Pallas kernels: 54.2 us -> 52.3 us  [shards(): pl.pallas_call(kernel, out_shape=jax.ShapeDtypeStruct((2, 2 * N, 512), BF...]
    reshape x1 -> x0, local copies, waits for them, and re-layouts: 0.66 us -> none  [shards(): return pieces.transpose(3, 1, 0, 2, 4).reshape(2, 2 * N, 512)]
    unnamed x0 -> x1, local copies, waits for them, and re-layouts: none -> 0.63 us
where the time goes in v5:
time: 53.1 us; the launch traced here: 53 us
  Pallas kernels  52.3 us (98%)
  local copies, waits for them, and re-layouts  0.63 us (1%)
    pallas_call x1, Pallas kernels, shards(): pl.pallas_call(kernel, out_shape=jax.ShapeDtypeStruct((2, 2 * N, 512), BF...  52.3 us

profile of v5, /device:TPU:1, one launch (start us, length us, event | category | flops | bytes accessed | tf_op | source)
XLA Modules:
  0.0 53.0 jit_solution(3227143453117415019)
XLA Ops:
  0.0 52.3 %layer.1 = bf16[2,32,512]{2,1,0:T(8,128)(2,1)S(1)} custom-call(s32[2]{0:T(128)} %len_hbm.1, bf16[2,2,4096]{2,1,0:T(2,128)(2,1)} %q_hbm.1, bf16[2,2,512]{2,1,0:T(2,128)(2,1)} %nk_hbm.1, bf16[2,2,512]{2,1,0:T(2,128)(2,1)} %nv_hbm.1, bf16[2,384,512]{2,1,0:T(8,128)(2,1)} %k_hbm.1, bf16[2,384,512]{2,1,0:T(8,128)(2,1)} %v_hbm.1, bf16[2,32,512]{2,1,0:T(8,128)(2,1)} %res_hbm.1, ...), custom_call_target="tpu_custom_call" | custom-call | tf_op jit(solution)/shard_map/layer/pallas_call | solution.py:427
  52.3 0.6 %copy.14 = bf16[2,32,512]{2,1,0:T(8,128)(2,1)} copy(bf16[2,32,512]{2,1,0:T(8,128)(2,1)S(1)} %layer.1) | data formatting | bytes 131072

commit v6 on v5

--- a/solution.py
+++ b/solution.py
@@ -24,7 +24,7 @@
     out_ref,
     len_ref, q_v, nk_v, nv_v, k_v, v_v, res_v, ow_v, gain_v, gw_v, uw_v, dw_v,
     qbd, heads, res_s, mid_t,
-    st_a, rc_a, st_b, rc_b, st_c, rc_c, st_e32, st_e, rc_e, st_f, rc_f, f32f, st_p, rc_p, kept, st_g, rc_g, both, order,
+    st_a32, st_a, rc_a, st_b, rc_b, st_c, rc_c, st_e32, st_e, rc_e, st_f, rc_f, f32f, st_g, rc_g, st_x, rc_x, both, order,
     load_sem, send_sem, recv_sem, met_sem,
 ):
     s = lax.axis_index("side")
@@ -34,7 +34,9 @@
     barrier = pltpu.get_barrier_semaphore()
 
     odd = lax.rem(c, 2)
-    partner = c + 1 - 2 * odd
+    plane = c // 8
+    lane = lax.rem(c, 8)
+    across = 2 * s + plane
 
     def greet_row(i, _):
         pl.semaphore_signal(
@@ -170,7 +172,7 @@
     )
     live = c * SPAN + lax.broadcasted_iota(jnp.int32, scores.shape, 1) < len_ref[s]
     scores = jnp.where(live, scores, VERY_LOW)
-    peak = jnp.max(scores, axis=1, keepdims=True)
+    peak = jnp.max(scores, axis=1, keepdims=True).astype(BF16).astype(F32)
     weights = jnp.where(live, jnp.exp(scores - peak), 0.0)
     total = jnp.sum(weights, axis=1, keepdims=True)
     loads[2].wait()
@@ -179,12 +181,13 @@
     stats = jnp.where(low_lane, peak, total)
     for o in range(N):
         g = o // 4
-        st_a[8 * o : 8 * o + 4, :] = summed[4 * o : 4 * o + 4, g * HD : (g + 1) * HD]
-        st_a[8 * o + 4 : 8 * o + 8, :] = stats[4 * o : 4 * o + 4, :]
-
+        st_a32[8 * o : 8 * o + 4, :] = summed[4 * o : 4 * o + 4, g * HD : (g + 1) * HD]
+        st_a32[8 * o + 4 : 8 * o + 8, :] = stats[4 * o : 4 * o + 4, :]
+
+    st_a[...] = st_a32[...].reshape(N, 8, HD).astype(BF16)
     met_columns()
-    to_columns(0, lambda peer: rows_at(st_a, peer, 8), rows_at(rc_a, c, 8))
-    rows_at(rc_a, c, 8)[...] = rows_at(st_a, c, 8)[...]
+    to_columns(0, lambda peer: st_a.at[peer], rc_a.at[c])
+    rc_a[c] = st_a[c]
 
     group_lanes = pl.ds(pl.multiple_of((c // 4) * HD, HD), HD)
     for copy in loads[3:8]:
@@ -207,8 +210,8 @@
     )
     gains = gain_v[...].astype(F32).reshape(1, 512)
 
-    arrived(0, rc_a.at[pl.ds(0, 8 * (N - 1))])
-    blocks = rc_a[...].reshape(N, 8, HD)
+    arrived(0, rc_a.at[pl.ds(0, N - 1)])
+    blocks = rc_a[...].astype(F32)
     sums, stat = blocks[:, 0:4, :], blocks[:, 4:8, :]
     low = lax.broadcasted_iota(jnp.int32, (N, 4, HD), 2) < HD // 2
     turned = pltpu.roll(stat, HD // 2, 2)
@@ -274,15 +277,11 @@
             send(9, rows_at(st_e, p, 32), rows_at(rc_e, p, 32), (s, owner, c))
 
         each(4 * k, 4 * k + (4 if k < 3 else 3), one)
-        half = own_half(mid)
         at = 4 * s + 3 - k
         for t in range(2):
             for i in range(4):
-                mid_t[at, 4 * t + 3 - i : 4 * t + 4 - i, :] = half[4 * t + i : 4 * t + i + 1, :]
+                mid_t[at, 4 * t + 3 - i : 4 * t + 4 - i, :] = mid[4 * t + i : 4 * t + i + 1, :]
         send(22, mid_t.at[at], mid_t.at[at], (1 - s, r, c))
-
-    def own_half(value):
-        return jnp.where(odd == 0, value[:, :256], value[:, 256:])
 
     arrived(1, rc_b.at[pl.ds(0, 3)])
     project(0)
@@ -339,60 +338,56 @@
             axis=0,
         )
         part = jnp.dot(act.astype(BF16), dw_v[...], preferred_element_type=F32)
-        st_p[k] = jnp.where(odd == 0, part[:, 256:], part[:, :256])
-        send(14 + k, st_p.at[k], rc_p.at[k], (s, r, partner))
-        kept[k] = own_half(part)
-
-    spot = s * (N // 2) + c // 2
-
-    def merge(k):
-        st_g[k] = (kept[k] + rc_p[k]).astype(BF16)
+        st_g[k] = part.astype(BF16)
 
         def one(i):
-            other = lax.rem(spot + i, N)
-            peer = (other // (N // 2), r, 2 * lax.rem(other, N // 2) + odd)
-            send(18 + k, st_g.at[k], rc_g.at[k, spot], peer)
-
-        each(1, N, one)
-        rc_g[k, spot] = st_g[k]
+            send(14 + k, st_g.at[k], rc_g.at[k, lane], (s, r, 8 * plane + lax.rem(lane + i, 8)))
+
+        each(1, 8, one)
+        rc_g[k, lane] = st_g[k]
+
+    def hand_on(k):
+        st_x[k] = jnp.sum(rc_g[k].astype(F32), axis=0).astype(BF16)
+        for i in (2, 1, 3):
+            other = lax.rem(across + i, 4)
+            send(18 + k, st_x.at[k], rc_x.at[k, across], (other // 2, r, 8 * lax.rem(other, 2) + lane))
+        rc_x[k, across] = st_x[k]
 
     def finish(k):
         for side in range(2):
-            parts = jnp.sum(rc_g[k, 8 * side : 8 * side + 8].astype(F32), axis=0)
-            both[odd, k, side] = (mid_t[4 * side + k] + parts).astype(BF16)
-        send(23, both.at[odd, k], both.at[odd, k], (s, r, partner))
+            parts = rc_x[k, 2 * side].astype(F32) + rc_x[k, 2 * side + 1].astype(F32)
+            both[k, side] = (mid_t[4 * side + k] + parts).astype(BF16)
 
     arrived(10, rc_f.at[pl.ds(0, 48)])
     down(0)
     arrived(11, rc_f.at[pl.ds(0, 64)])
     down(1)
-    arrived(14, rc_p.at[0])
-    merge(0)
     arrived(12, rc_f.at[pl.ds(0, 64)])
     down(2)
-    arrived(15, rc_p.at[1])
-    merge(1)
     arrived(13, rc_f.at[pl.ds(0, 64)])
     down(3)
-    arrived(16, rc_p.at[2])
-    merge(2)
-    arrived(17, rc_p.at[3])
-    merge(3)
+    arrived(14, rc_g.at[0, pl.ds(0, 7)])
+    hand_on(0)
+    arrived(15, rc_g.at[1, pl.ds(0, 7)])
+    hand_on(1)
+    arrived(16, rc_g.at[2, pl.ds(0, 7)])
+    hand_on(2)
+    arrived(17, rc_g.at[3, pl.ds(0, 7)])
+    hand_on(3)
     arrived(22, mid_t.at[pl.ds(0, 4)])
-    arrived(18, rc_g.at[0, pl.ds(0, N - 1)])
+    arrived(18, rc_x.at[0, pl.ds(0, 3)])
     finish(0)
-    arrived(19, rc_g.at[1, pl.ds(0, N - 1)])
+    arrived(19, rc_x.at[1, pl.ds(0, 3)])
     finish(1)
-    arrived(20, rc_g.at[2, pl.ds(0, N - 1)])
+    arrived(20, rc_x.at[2, pl.ds(0, 3)])
     finish(2)
-    arrived(21, rc_g.at[3, pl.ds(0, N - 1)])
+    arrived(21, rc_x.at[3, pl.ds(0, 3)])
     finish(3)
-    arrived(23, both.at[0])
-    rows = jnp.concatenate([both[h].astype(F32).reshape(4 * N, 256) for h in range(2)], axis=1)
-    result = jnp.dot(order[...], rows.astype(BF16), preferred_element_type=F32)
+    rows = both[...].astype(F32).reshape(4 * N, 512).astype(BF16)
+    result = jnp.dot(order[...], rows, preferred_element_type=F32)
     out_ref[...] = result.astype(BF16).reshape(2, 2 * N, 512)
 
-    sent(0, rc_a.at[pl.ds(0, 8 * (N - 1))])
+    sent(0, rc_a.at[pl.ds(0, N - 1)])
     sent(1, rc_b.at[pl.ds(0, 3)])
     sent(2, rc_b.at[pl.ds(0, 4)])
     sent(3, rc_b.at[pl.ds(0, 4)])
@@ -406,16 +401,15 @@
     sent(11, rc_f.at[pl.ds(0, 64)])
     sent(12, rc_f.at[pl.ds(0, 64)])
     sent(13, rc_f.at[pl.ds(0, 64)])
-    sent(14, rc_p.at[0])
-    sent(15, rc_p.at[1])
-    sent(16, rc_p.at[2])
-    sent(17, rc_p.at[3])
-    sent(18, rc_g.at[0, pl.ds(0, N - 1)])
-    sent(19, rc_g.at[1, pl.ds(0, N - 1)])
-    sent(20, rc_g.at[2, pl.ds(0, N - 1)])
-    sent(21, rc_g.at[3, pl.ds(0, N - 1)])
+    sent(14, rc_g.at[0, pl.ds(0, 7)])
+    sent(15, rc_g.at[1, pl.ds(0, 7)])
+    sent(16, rc_g.at[2, pl.ds(0, 7)])
+    sent(17, rc_g.at[3, pl.ds(0, 7)])
+    sent(18, rc_x.at[0, pl.ds(0, 3)])
+    sent(19, rc_x.at[1, pl.ds(0, 3)])
+    sent(20, rc_x.at[2, pl.ds(0, 3)])
+    sent(21, rc_x.at[3, pl.ds(0, 3)])
     sent(22, mid_t.at[pl.ds(0, 4)])
-    sent(23, both.at[0])
 
 
 def shards(query, new_keys, new_values, key_cache, value_cache, lengths, residual, out_weight,
@@ -445,19 +439,19 @@
             vm(64, 512),
             vm(N, 4, HD),
             vm(2 * N, 512),
-            vm(8, 8, 256),
-            vm(8 * N, HD), vm(8 * N, HD),
+            vm(8, 8, 512),
+            vm(8 * N, HD), vm(N, 8, HD, kind=BF16), vm(N, 8, HD, kind=BF16),
             vm(4, HD), vm(N, 4, HD),
             vm(4, 8, 512, kind=BF16), vm(4, N, 8, 512, kind=BF16),
             vm(32 * N, HD), vm(32 * N, HD, kind=BF16), vm(32 * N, HD, kind=BF16),
             vm(16, HD, kind=BF16), vm(16 * N, HD, kind=BF16), vm(16 * N, HD),
-            vm(4, 8, 256), vm(4, 8, 256), vm(4, 8, 256),
-            vm(4, 8, 256, kind=BF16), vm(4, N, 8, 256, kind=BF16),
-            vm(2, 4, 2, 8, 256, kind=BF16),
+            vm(4, 8, 512, kind=BF16), vm(4, 8, 8, 512, kind=BF16),
+            vm(4, 8, 512, kind=BF16), vm(4, 4, 8, 512, kind=BF16),
+            vm(4, 2, 8, 512, kind=BF16),
             vm(4 * N, 4 * N, kind=BF16),
             pltpu.SemaphoreType.DMA((12,)),
-            pltpu.SemaphoreType.DMA((24,)),
-            pltpu.SemaphoreType.DMA((24,)),
+            pltpu.SemaphoreType.DMA((23,)),
+            pltpu.SemaphoreType.DMA((23,)),
             pltpu.SemaphoreType.REGULAR,
         ],
         compiler_params=pltpu.CompilerParams(

time: 53.1 us -> 52.1 us (0.981)
  Pallas kernels: 52.3 us -> 51.3 us
    pallas_call x1, Pallas kernels: 52.3 us -> 51.3 us  [shards(): pl.pallas_call(kernel, out_shape=jax.ShapeDtypeStruct((2, 2 * N, 512), BF...]
where the time goes in v6:
time: 52.1 us; the launch traced here: 52 us
  Pallas kernels  51.3 us (98%)
  local copies, waits for them, and re-layouts  0.63 us (1%)
    pallas_call x1, Pallas kernels, shards(): pl.pallas_call(kernel, out_shape=jax.ShapeDtypeStruct((2, 2 * N, 512), BF...  51.3 us

profile of v6, /device:TPU:1, one launch (start us, length us, event | category | flops | bytes accessed | tf_op | source)
XLA Modules:
  0.0 52.0 jit_solution(593880976090859039)
XLA Ops:
  0.0 51.3 %layer.1 = bf16[2,32,512]{2,1,0:T(8,128)(2,1)S(1)} custom-call(s32[2]{0:T(128)} %len_hbm.1, bf16[2,2,4096]{2,1,0:T(2,128)(2,1)} %q_hbm.1, bf16[2,2,512]{2,1,0:T(2,128)(2,1)} %nk_hbm.1, bf16[2,2,512]{2,1,0:T(2,128)(2,1)} %nv_hbm.1, bf16[2,384,512]{2,1,0:T(8,128)(2,1)} %k_hbm.1, bf16[2,384,512]{2,1,0:T(8,128)(2,1)} %v_hbm.1, bf16[2,32,512]{2,1,0:T(8,128)(2,1)} %res_hbm.1, ...), custom_call_target="tpu_custom_call" | custom-call | tf_op jit(solution)/shard_map/layer/pallas_call | solution.py:421
  51.3 0.6 %copy.14 = bf16[2,32,512]{2,1,0:T(8,128)(2,1)} copy(bf16[2,32,512]{2,1,0:T(8,128)(2,1)S(1)} %layer.1) | data formatting | bytes 131072

commit v7 on v6

--- a/solution.py
+++ b/solution.py
@@ -57,7 +57,6 @@
         pl.semaphore_signal(barrier, inc=1, device_id=(1 - s, r, 2 * i + 1), device_id_type=MESH)
         return 0
 
-    lax.fori_loop(0, N - 1, greet_row, 0)
 
     @pl.when(odd == 1)
     def _():
@@ -69,6 +68,7 @@
     def _():
         pl.semaphore_signal(barrier, inc=1, device_id=(s, r, c + 1), device_id_type=MESH)
 
+    lax.fori_loop(0, N - 1, greet_row, 0)
     lax.fori_loop(0, N // 2, greet_side, 0)
 
     loads = [
@@ -281,7 +281,6 @@
         for t in range(2):
             for i in range(4):
                 mid_t[at, 4 * t + 3 - i : 4 * t + 4 - i, :] = mid[4 * t + i : 4 * t + i + 1, :]
-        send(22, mid_t.at[at], mid_t.at[at], (1 - s, r, c))
 
     arrived(1, rc_b.at[pl.ds(0, 3)])
     project(0)
@@ -319,6 +318,8 @@
     for k in range(3, -1, -1):
         give_act(k)
     rc_f[0:16, :] = st_f[...]
+    for k in range(4):
+        send(22, mid_t.at[4 * s + k], mid_t.at[4 * s + k], (1 - s, r, c))
     target = lax.broadcasted_iota(jnp.int32, (4 * N, 4 * N), 0)
     source = lax.broadcasted_iota(jnp.int32, (4 * N, 4 * N), 1)
     row = lax.rem(r + N // 2 + offset(source // 16 * 4 + lax.rem(source, 4)), N)

time: 52.1 us -> 51.9 us (level)
  no operation moved by 1% of the time
where the time goes in v7:
time: 51.9 us; the launch traced here: 51.8 us
  Pallas kernels  51.2 us (99%)
  local copies, waits for them, and re-layouts  0.63 us (1%)
    pallas_call x1, Pallas kernels, shards(): pl.pallas_call(kernel, out_shape=jax.ShapeDtypeStruct((2, 2 * N, 512), BF...  51.2 us

profile of v7, /device:TPU:1, one launch (start us, length us, event | category | flops | bytes accessed | tf_op | source)
XLA Modules:
  0.0 51.8 jit_solution(13909441947643861464)
XLA Ops:
  0.0 51.2 %layer.1 = bf16[2,32,512]{2,1,0:T(8,128)(2,1)S(1)} custom-call(s32[2]{0:T(128)} %len_hbm.1, bf16[2,2,4096]{2,1,0:T(2,128)(2,1)} %q_hbm.1, bf16[2,2,512]{2,1,0:T(2,128)(2,1)} %nk_hbm.1, bf16[2,2,512]{2,1,0:T(2,128)(2,1)} %nv_hbm.1, bf16[2,384,512]{2,1,0:T(8,128)(2,1)} %k_hbm.1, bf16[2,384,512]{2,1,0:T(8,128)(2,1)} %v_hbm.1, bf16[2,32,512]{2,1,0:T(8,128)(2,1)} %res_hbm.1, ...), custom_call_target="tpu_custom_call" | custom-call | tf_op jit(solution)/shard_map/layer/pallas_call | solution.py:422
  51.2 0.6 %copy.14 = bf16[2,32,512]{2,1,0:T(8,128)(2,1)} copy(bf16[2,32,512]{2,1,0:T(8,128)(2,1)S(1)} %layer.1) | data formatting | bytes 131072
